TPU v7x, 512 devices: a whole 4x4x16 slice. The times are simulated.
512 devices in a mesh: ctx: 64 (over z, y), tp: 8 (over x, core).
Axes of the slice: x: 4, y: 4, z: 16, core: 2. Of those that a mesh axis runs over, the one named last changes fastest.
Arguments:
- queries: bfloat16 [16384, 32, 128], P('ctx', 'tp'), may hold values from -6 to 6
- keys: bfloat16 [16384, 32, 128], P('ctx', 'tp'), may hold values from -6 to 6
- values: bfloat16 [16384, 32, 128], P('ctx', 'tp'), may hold values from -6 to 6
- init_state: float32 [32, 128, 128], P('tp'), may hold values from -192 to 192
- gain: float32 [32, 128], P('tp'), may hold values from 0.1 to 1.9
- cotangent: bfloat16 [16384, 32, 128], P('ctx', 'tp'), may hold values from -6 to 6
Outputs:
- normed: bfloat16 [16384, 32, 128], P('ctx', 'tp')
- d_query: bfloat16 [16384, 32, 128], P('ctx', 'tp')
- d_key: bfloat16 [16384, 32, 128], P('ctx', 'tp')
- d_value: bfloat16 [16384, 32, 128], P('ctx', 'tp')
- d_state: float32 [32, 128, 128], P('tp')
- d_gain: float32 [32, 128], P('tp')
All inputs are finite; a program needn't handle non-finite values.
Results may differ from a plain program's by a relative error of at most 0.005.
Values sent between devices are 32-bit elements; how exact they have to be, the bound alone decides.
No kernel may reach another device: no remote copies, remote signals or barrier semaphores. Data moves between devices by JAX's collectives and lax.ppermute only.
A program may use at most 64 MiB of HBM per device.

v0:
```python
import jax
import jax.numpy as jnp
from jax import lax
from jax.sharding import PartitionSpec as P

BLK = 256


HIGH = lax.Precision.HIGHEST


def carried_in(array, axis, combine, identity, reverse):
    peers, position = (lax.axis_size(axis), lax.axis_index(axis))
    everything = lax.all_gather(array, axis)
    start = jnp.broadcast_to(jnp.asarray(identity, array.dtype), array.shape)

    def step(k, before):
        at = peers - 1 - k if reverse else k
        reached = at > position if reverse else at < position
        new = combine(before, everything[at])
        return jnp.where(reached, new, before)

    return lax.fori_loop(0, peers, step, start)


def add_states(earlier, later):
    return earlier + later


def before_sums(stack):
    zero_one = jnp.zeros_like(stack)
    return jnp.concatenate([zero_one, jnp.cumsum(stack[:-1], axis=0)], axis=0)


def after_sums(stack):
    zero_one = jnp.zeros_like(stack)
    return jnp.concatenate(
        [jnp.flip(jnp.cumsum(jnp.flip(stack[1:], 0), axis=0), 0), zero_one], axis=0
    )


def on_device(queries, keys, values, init_state, gain, cotangent):
    count = queries.shape[0]
    heads = queries.shape[1]
    width = queries.shape[2]
    nblocks = count // BLK
    width_total = heads * lax.axis_size("tp") * width
    rows = jnp.arange(BLK)
    causal = (rows[:, None] >= rows[None, :])[None, None]
    query_b = queries.reshape(nblocks, BLK, heads, width)
    key_b = keys.reshape(nblocks, BLK, heads, width)
    value_b = values.reshape(nblocks, BLK, heads, width)
    scores = jnp.einsum("bihd,bjhd->bhij", query_b, key_b, preferred_element_type=jnp.float32)
    scores = jnp.where(causal, scores, 0.0).astype(jnp.bfloat16)
    sub_state = jnp.einsum("bjhd,bjhe->bhde", key_b, value_b, preferred_element_type=jnp.float32)
    own_state = jnp.sum(sub_state, axis=0)
    earlier = carried_in(own_state, "ctx", add_states, jnp.zeros_like(own_state), False)
    state_before = init_state[None] + earlier[None] + before_sums(sub_state)
    attn = jnp.einsum("bhij,bjhe->bihe", scores, value_b, preferred_element_type=jnp.float32)
    attn = attn + jnp.einsum(
        "bihd,bhde->bihe", query_b.astype(jnp.float32), state_before, precision=HIGH
    )
    attn = attn.reshape(count, heads, width)
    cot_wide = cotangent.astype(jnp.float32)
    local_ssq = jnp.sum(attn * attn, axis=(1, 2))
    local_dot = jnp.sum(gain * cot_wide * attn, axis=(1, 2))
    ssq, gdot = lax.psum((local_ssq, local_dot), "tp")
    rscale = lax.rsqrt(ssq / width_total + 1e-06)[:, None, None]
    normed = (attn * rscale * gain).astype(jnp.bfloat16)
    d_attn = (
        rscale * gain * cot_wide - attn * rscale**3 * gdot[:, None, None] / width_total
    ).astype(jnp.bfloat16)
    gain_term = jnp.sum(cot_wide * attn * rscale, axis=0)
    d_attn_b = d_attn.reshape(nblocks, BLK, heads, width)
    back = jnp.einsum("bihe,bjhe->bhij", d_attn_b, value_b, preferred_element_type=jnp.float32)
    back = jnp.where(causal, back, 0.0).astype(jnp.bfloat16)
    sub_grad = jnp.einsum("bihd,bihe->bhde", query_b, d_attn_b, preferred_element_type=jnp.float32)
    own_grad = jnp.sum(sub_grad, axis=0)
    d_state, d_gain = lax.psum((own_grad, gain_term), "ctx")
    later = carried_in(own_grad, "ctx", add_states, jnp.zeros_like(own_grad), True)
    grad_after = later[None] + after_sums(sub_grad)
    d_query = jnp.einsum("bhij,bjhd->bihd", back, key_b, preferred_element_type=jnp.float32)
    d_query = d_query + jnp.einsum(
        "bihe,bhde->bihd", d_attn_b.astype(jnp.float32), state_before, precision=HIGH
    )
    d_key = jnp.einsum("bhij,bihd->bjhd", back, query_b, preferred_element_type=jnp.float32)
    d_key = d_key + jnp.einsum(
        "bjhe,bhde->bjhd", value_b.astype(jnp.float32), grad_after, precision=HIGH
    )
    d_value = jnp.einsum("bhij,bihe->bjhe", scores, d_attn_b, preferred_element_type=jnp.float32)
    d_value = d_value + jnp.einsum(
        "bjhd,bhde->bjhe", key_b.astype(jnp.float32), grad_after, precision=HIGH
    )
    return (
        normed,
        d_query.reshape(count, heads, width).astype(jnp.bfloat16),
        d_key.reshape(count, heads, width).astype(jnp.bfloat16),
        d_value.reshape(count, heads, width).astype(jnp.bfloat16),
        d_state,
        d_gain,
    )


def solution(mesh):
    placed = (
        P("ctx", "tp", None),
        P("ctx", "tp", None),
        P("ctx", "tp", None),
        P("tp", None, None),
        P("tp", None),
        P("ctx", "tp", None),
    )
    return jax.shard_map(
        on_device,
        mesh=mesh,
        in_specs=placed,
        out_specs=(
            P("ctx", "tp", None),
            P("ctx", "tp", None),
            P("ctx", "tp", None),
            P("ctx", "tp", None),
            P("tp", None, None),
            P("tp", None),
        ),
        check_vma=False,
    )
```

profile of v0, /device:TPU:24, one launch (start us, length us, event | category | flops | bytes accessed | tf_op | source)
XLA Modules:
  0.0 839.2 jit_solution(15062239145370570101)
XLA Ops:
  8.1 1.9 fusion.18
  10.1 1.1 copy.45
  11.2 1.3 fusion
  12.9 194.5 %all-gather.5.cloned.1.call-done = f32[256,128,128]{2,1,0:T(8,128)} async-done(((f32[4,128,128]{2,1,0:T(8,128)}), f32[256,128,128]{2,1,0:T(8,128)}) %all-gather.5.cloned.1.call-update) | async-done | bytes 16777232 | tf_op jit(solution)/shard_map/all_gather | solution.py:14
  207.4 68.1 %while.30 = (s32[]{:T(128)}, f32[4,128,128]{2,1,0:T(8,128)S(1)}, s32[]{:T(128)}, f32[64,4,128,128]{3,2,1,0:T(8,128)}, s32[]{:T(128)}, /*index=5*/s32[]{:T(128)}) while((s32[]{:T(128)}, f32[4,128,128]{2,1,0:T(8,128)S(1)}, s32[]{:T(128)}, f32[64,4,128,128]{3,2,1,0:T(8,128)}, s32[]{:T(128)}, /*index=5*/s32[]{:T(128)}) %tuple.91), condition=%wide.region_1.2_spmd.clone, body=%wide.region_0.1_spmd.clone.sunk | while | flops 196612 | bytes 786533 | solution.py:23
  208.5 1.0 add_select_fusion.4
  218.0 1.0 add_select_fusion.4
  220.2 1.0 add_select_fusion.4
  222.3 1.0 add_select_fusion.4
  224.4 1.0 add_select_fusion.4
  226.5 1.0 add_select_fusion.4
  228.7 1.0 add_select_fusion.4
  238.2 1.0 add_select_fusion.4
  240.4 1.0 add_select_fusion.4
  276.5 1.4 multiply_reduce_fusion
  277.9 14.1 %psum.28 = f32[256]{0:T(256)S(1)} all-reduce(f32[256]{0:T(256)S(1)} %get-tuple-element.265), channel_id=1, replica_groups=mesh['ctx'=64,'tp'=8] {'tp'}, use_global_device_ids=true, to_apply=%region_3.4 | all-reduce | flops 256 | bytes 2048 | tf_op jit(solution)/shard_map/psum | solution.py:67
  293.0 12.4 %psum.29 = f32[256]{0:T(256)S(1)} all-reduce(f32[256]{0:T(256)S(1)} %get-tuple-element.244), channel_id=1, replica_groups=mesh['ctx'=64,'tp'=8] {'tp'}, use_global_device_ids=true, to_apply=%region_5.6 | all-reduce | flops 256 | bytes 2048 | tf_op jit(solution)/shard_map/psum | solution.py:67
  306.3 1.2 convolution_bitcast_fusion.3
  311.0 1.2 convolution_bitcast_fusion.1
  313.6 137.0 %psum.31 = f32[4,128]{1,0:T(4,128)} all-reduce(f32[4,128]{1,0:T(4,128)S(1)} %get-tuple-element.243), channel_id=1, replica_groups=mesh['ctx'=64,'tp'=8] {'ctx'}, use_global_device_ids=true, to_apply=%region_10.11 | all-reduce | flops 512 | bytes 4096 | tf_op jit(solution)/shard_map/psum | solution.py:79
  451.2 118.7 %all-reduce.2.cloned.1.call-done = f32[4,128,128]{1,2,0:T(8,128)} async-done(((f32[4,128,128]{1,2,0:T(8,128)}), f32[4,128,128]{1,2,0:T(8,128)}) %all-reduce.2.cloned.1.call-update) | async-done | bytes 262160 | tf_op jit(solution)/shard_map/psum | solution.py:79
  569.9 1.8 copy.63
  571.7 190.0 %all-gather.7.cloned.1.call-done = f32[256,128,128]{2,1,0:T(8,128)} async-done(((f32[4,128,128]{2,1,0:T(8,128)}), f32[256,128,128]{2,1,0:T(8,128)}) %all-gather.7.cloned.1.call-update) | async-done | bytes 16777232 | tf_op jit(solution)/shard_map/all_gather | solution.py:14
  761.7 68.4 %while.31 = (s32[]{:T(128)}, f32[4,128,128]{2,1,0:T(8,128)S(1)}, s32[]{:T(128)}, f32[64,4,128,128]{3,2,1,0:T(8,128)}, s32[]{:T(128)}, /*index=5*/s32[]{:T(128)}, s32[]{:T(128)}, s32[]{:T(128)}) while((s32[]{:T(128)}, f32[4,128,128]{2,1,0:T(8,128)S(1)}, s32[]{:T(128)}, f32[64,4,128,128]{3,2,1,0:T(8,128)}, s32[]{:T(128)}, ...), condition=%wide.region_7.8_spmd.clone, body=%wide.region_6.7_spmd.clone.sunk | while | flops 196616 | bytes 786595 | solution.py:23
  (152 shorter events, 135.9 us)
Async XLA Ops:
  7.2 1.0 copy-start
  7.2 822.9 %copy-start.1 = (bf16[256,4,128]{2,1,0:T(4,128)(2,1)S(1)}, bf16[256,4,128]{2,1,0:T(4,128)(2,1)}, u32[]{:S(2)}) copy-start(bf16[256,4,128]{2,1,0:T(4,128)(2,1)} %param.11) | copy-start | bytes 786436
  7.2 443.7 %copy-start.2 = (bf16[256,4,128]{2,1,0:T(4,128)(2,1)S(1)}, bf16[256,4,128]{2,1,0:T(4,128)(2,1)}, u32[]{:S(2)}) copy-start(bf16[256,4,128]{2,1,0:T(4,128)(2,1)} %param.10) | copy-start | bytes 786436
  7.2 200.2 %all-gather.5.cloned.1.call-start = ((), (), s32[]{:S(2)}) async-start(), calls=%async_computation.1 | async-start | bytes 17039360 | tf_op jit(solution)/shard_map/all_gather | solution.py:14
  307.4 0.9 copy-start.3
  308.3 261.6 %all-reduce.2.cloned.1.call-start = ((), (), s32[]{:S(2)}) async-start(), calls=%async_computation | async-start | bytes 524288 | tf_op jit(solution)/shard_map/psum | solution.py:79
  309.0 452.6 %all-gather.7.cloned.1.call-start = ((), (), s32[]{:S(2)}) async-start(), calls=%async_computation.2 | async-start | bytes 17039360 | tf_op jit(solution)/shard_map/all_gather | solution.py:14
Sparse Core Ops, SparseCore 0:
  11.6 195.7 all-gather.4
  313.1 256.7 all-reduce.1
  573.8 187.7 all-gather.6
where the time goes:
time: 846 us; the launch traced here: 839 us
  waiting for transfers between devices  505 us (60%)
  blocking collectives  164 us (19%)
  other arithmetic  136 us (16%)
  between operations  13.9 us (2%)
  matrix products  9.54 us (1%)
    all_gather x2, waiting for transfers between devices, carried_in(): everything = lax.all_gather(array, axis)  384 us
    psum x1, blocking collectives, on_device(): d_state, d_gain = lax.psum((own_grad, gain_term), 'ctx')  137 us
    select_n x128, other arithmetic, step(): return jnp.where(reached, new, before)  133 us
    psum x1, waiting for transfers between devices, on_device(): d_state, d_gain = lax.psum((own_grad, gain_term), 'ctx')  119 us
    psum x2, blocking collectives, on_device(): ssq, gdot = lax.psum((local_ssq, local_dot), 'tp')  26.5 us
  transfers between devices with their start and end apart: 3, of which 3 were waited for; matrix products, arithmetic and copies ran while one was open for 1% of the time, Pallas kernels for 0%

commit v1 on v0

v1 whole, which is shorter than its diff:
```python
import functools

import jax
import jax.numpy as jnp
from jax import lax
from jax.experimental import pallas as pl
from jax.experimental.pallas import tpu as pltpu
from jax.sharding import PartitionSpec as P

F32 = jnp.float32
BF16 = jnp.bfloat16
EPS = 1e-06
NN = (((1,), (0,)), ((), ()))
NT = (((1,), (1,)), ((), ()))
TN = (((0,), (0,)), ((), ()))


def dot(a, b, dims):
    return lax.dot_general(a, b, dims, preferred_element_type=F32)


def split(a):
    high = a.astype(BF16)
    return high, (a - high.astype(F32)).astype(BF16)


def times(a, m, turned):
    high, low = split(m)
    both = jnp.concatenate([high, low], axis=1 if turned else 0)
    return dot(jnp.concatenate([a, a], axis=1), both, NT if turned else NN)


def head_rows(h, tokens, heads):
    return pl.ds(h, tokens, stride=heads)


def causal(tokens):
    rows = lax.broadcasted_iota(jnp.int32, (tokens, tokens), 0)
    cols = lax.broadcasted_iota(jnp.int32, (tokens, tokens), 1)
    return rows >= cols


def state_kernel(k_ref, v_ref, state_ref, kh_ref, vh_ref, k32, v32):
    heads, tokens, _ = kh_ref.shape
    k32[...] = k_ref[...].astype(F32)
    v32[...] = v_ref[...].astype(F32)
    for h in range(heads):
        k = k32[head_rows(h, tokens, heads), :].astype(BF16)
        v = v32[head_rows(h, tokens, heads), :].astype(BF16)
        state_ref[h] = dot(k, v, TN)
        kh_ref[h] = k
        vh_ref[h] = v


def local_kernel(q_ref, kh_ref, vh_ref, qh_ref, scores_ref, attn_ref, q32):
    heads, tokens, _ = kh_ref.shape
    q32[...] = q_ref[...].astype(F32)
    keep = causal(tokens)
    for h in range(heads):
        q = q32[head_rows(h, tokens, heads), :].astype(BF16)
        qh_ref[h] = q
        scores = jnp.where(keep, dot(q, kh_ref[h], NT), 0.0).astype(BF16)
        scores_ref[h] = scores
        attn_ref[h] = dot(scores, vh_ref[h], NN)


def cot_kernel(c_ref, gain_ref, ch_ref, c32):
    heads, tokens, _ = ch_ref.shape
    c32[...] = c_ref[...].astype(F32)
    for h in range(heads):
        ch_ref[h] = c32[head_rows(h, tokens, heads), :]


def prefix_kernel(x_ref, out_ref):
    peers = x_ref.shape[0]
    total = jnp.zeros(x_ref.shape[1:], F32)
    for i in range(peers):
        out_ref[i] = total
        total = total + x_ref[i]


def suffix_kernel(x_ref, out_ref):
    peers, rows = x_ref.shape[:2]
    total = jnp.zeros(x_ref.shape[1:], F32)
    for i in reversed(range(peers)):
        out_ref[i, :rows] = total
        total = total + x_ref[i]
    for i in range(peers):
        out_ref[i, rows:] = total


def attn_kernel(before_ref, init_ref, qh_ref, local_ref, ch_ref, gain_ref, attn_ref, state_ref, stats_ref):
    heads, tokens, width = qh_ref.shape
    ssq = jnp.zeros((tokens, width), F32)
    gdot = jnp.zeros((tokens, width), F32)
    for h in range(heads):
        state = init_ref[h] + before_ref[h]
        state_ref[h] = state
        attn = local_ref[h] + times(qh_ref[h], state, False)
        attn_ref[h] = attn
        ssq = ssq + attn * attn
        gdot = gdot + gain_ref[h : h + 1, :] * ch_ref[h] * attn
    ssq_row = jnp.sum(ssq.T, axis=0, keepdims=True)
    gdot_row = jnp.sum(gdot.T, axis=0, keepdims=True)
    half = tokens // 2
    rows = jnp.concatenate(
        [ssq_row[:, :half], ssq_row[:, half:], gdot_row[:, :half], gdot_row[:, half:]], axis=0
    )
    for i in range(stats_ref.shape[0]):
        stats_ref[i] = rows


def grad_kernel(width_total, stats_ref, attn_ref, ch_ref, gain_ref, qh_ref, dh_ref, grad_ref, scale_ref):
    heads, tokens, width = qh_ref.shape
    rows = stats_ref[0]
    for i in range(1, stats_ref.shape[0]):
        rows = rows + stats_ref[i]
    ssq = jnp.concatenate([rows[0:1], rows[1:2]], axis=1)
    gdot = jnp.concatenate([rows[2:3], rows[3:4]], axis=1)
    rscale = lax.rsqrt(ssq / width_total + EPS)
    pull = rscale * rscale * rscale * gdot / width_total
    rscale = jnp.broadcast_to(rscale, (width, tokens)).T
    pull = jnp.broadcast_to(pull, (width, tokens)).T
    scale_ref[...] = rscale
    for h in range(heads):
        gain = gain_ref[h : h + 1, :]
        d_attn = (rscale * gain * ch_ref[h] - attn_ref[h] * pull).astype(BF16)
        dh_ref[h] = d_attn
        grad_ref[h] = dot(qh_ref[h], d_attn, TN)


def gain_kernel(attn_ref, ch_ref, gain_ref, scale_ref, normed_ref, term_ref, out32):
    heads, tokens, _ = ch_ref.shape
    rscale = scale_ref[...]
    terms = []
    for h in range(heads):
        scaled = attn_ref[h] * rscale
        out32[head_rows(h, tokens, heads), :] = scaled * gain_ref[h : h + 1, :]
        terms.append(jnp.sum(ch_ref[h] * scaled, axis=0, keepdims=True))
    normed_ref[...] = out32[...].astype(BF16)
    term = jnp.concatenate(terms, axis=0)
    for i in range(term_ref.shape[0]):
        term_ref[i] = term


def back_kernel(dh_ref, vh_ref, kh_ref, qh_ref, state_ref, scores_ref, dq_ref, dk_ref, dv_ref, out32):
    heads, tokens, _ = kh_ref.shape
    keep = causal(tokens)
    for h in range(heads):
        d_attn = dh_ref[h]
        back = jnp.where(keep, dot(d_attn, vh_ref[h], NT), 0.0).astype(BF16)
        d_query = dot(back, kh_ref[h], NN) + times(d_attn, state_ref[h], True)
        out32[head_rows(h, tokens, heads), :] = d_query
        dk_ref[h] = dot(back, qh_ref[h], TN)
        dv_ref[h] = dot(scores_ref[h], d_attn, TN)
    dq_ref[...] = out32[...].astype(BF16)


def last_kernel(after_ref, kh_ref, vh_ref, dk_in, dv_in, dk_ref, dv_ref, k32, v32):
    heads, tokens, _ = kh_ref.shape
    for h in range(heads):
        after = after_ref[h]
        k32[head_rows(h, tokens, heads), :] = dk_in[h] + times(vh_ref[h], after, True)
        v32[head_rows(h, tokens, heads), :] = dv_in[h] + times(kh_ref[h], after, False)
    dk_ref[...] = k32[...].astype(BF16)
    dv_ref[...] = v32[...].astype(BF16)


def sum_kernel(x_ref, out_ref):
    total = x_ref[0]
    for i in range(1, x_ref.shape[0]):
        total = total + x_ref[i]
    out_ref[...] = total


def call(kernel, name, outs, args, scratch=(), flops=0):
    moved = sum(a.size * a.dtype.itemsize for a in list(args) + list(outs))
    return pl.pallas_call(
        kernel,
        name=name,
        out_shape=outs,
        in_specs=[pl.BlockSpec(memory_space=pltpu.VMEM)] * len(args),
        out_specs=[pl.BlockSpec(memory_space=pltpu.VMEM)] * len(outs),
        scratch_shapes=scratch,
        compiler_params=pltpu.CompilerParams(vmem_limit_bytes=24 * 2**20),
        cost_estimate=pl.CostEstimate(flops=flops, bytes_accessed=moved, transcendentals=0),
    )(*args)


def shape(dims, dtype=F32):
    return jax.ShapeDtypeStruct(dims, dtype)


def on_device(queries, keys, values, init_state, gain, cotangent):
    tokens, heads, width = queries.shape
    peers = lax.axis_size("ctx")
    sharers = lax.axis_size("tp")
    width_total = heads * sharers * width
    flat = (tokens * heads, width)
    by_head = (heads, tokens, width)
    states = (heads, width, width)
    chunk = heads * width // peers
    chunks = (peers, chunk, width)
    squares = (heads, tokens, tokens)
    wide = pltpu.VMEM(flat, F32)
    unit = 2 * tokens * width * width * heads
    q, k, v, c = (a.reshape(flat) for a in (queries, keys, values, cotangent))

    own, kh, vh = call(
        state_kernel,
        "state",
        [shape(states), shape(by_head, BF16), shape(by_head, BF16)],
        [k, v],
        [wide, wide],
        unit,
    )
    gathered = lax.all_to_all(own.reshape(chunks), "ctx", 0, 0)
    qh, scores, local = call(
        local_kernel,
        "local",
        [shape(by_head, BF16), shape(squares, BF16), shape(by_head)],
        [q, kh, vh],
        [wide],
        4 * unit,
    )
    (before,) = call(prefix_kernel, "prefix", [shape(chunks)], [gathered])
    c, before = lax.optimization_barrier((c, before))
    before = lax.all_to_all(before, "ctx", 0, 0).reshape(states)
    (ch,) = call(cot_kernel, "cotangent", [shape(by_head)], [c, gain], [wide])
    attn, state, stats = call(
        attn_kernel,
        "attn",
        [shape(by_head), shape(states), shape((sharers, 4, tokens // 2))],
        [before, init_state, qh, local, ch, gain],
        (),
        2 * unit,
    )
    stats = lax.all_to_all(stats, "tp", 0, 0)
    dh, grad, scale = call(
        functools.partial(grad_kernel, width_total),
        "grad",
        [shape(by_head, BF16), shape(states), shape((tokens, width))],
        [stats, attn, ch, gain, qh],
        (),
        unit,
    )
    gathered = lax.all_to_all(grad.reshape(chunks), "ctx", 0, 0)
    normed, term = call(
        gain_kernel,
        "normed",
        [shape(flat, BF16), shape((peers, heads, width))],
        [attn, ch, gain, scale],
        [wide],
    )
    term = lax.all_to_all(term, "ctx", 0, 0)
    (after,) = call(suffix_kernel, "suffix", [shape((peers, 2 * chunk, width))], [gathered])
    dh, after = lax.optimization_barrier((dh, after))
    after = lax.all_to_all(after, "ctx", 0, 0)
    d_query, dk, dv = call(
        back_kernel,
        "back",
        [shape(flat, BF16), shape(by_head), shape(by_head)],
        [dh, vh, kh, qh, state, scores],
        [wide],
        10 * unit,
    )
    d_state = after[:, chunk:].reshape(states)
    after = after[:, :chunk].reshape(states)
    d_key, d_value = call(
        last_kernel,
        "last",
        [shape(flat, BF16), shape(flat, BF16)],
        [after, kh, vh, dk, dv],
        [wide, wide],
        4 * unit,
    )
    (d_gain,) = call(sum_kernel, "gain_sum", [shape((heads, width))], [term])
    whole = (tokens, heads, width)
    return (
        normed.reshape(whole),
        d_query.reshape(whole),
        d_key.reshape(whole),
        d_value.reshape(whole),
        d_state,
        d_gain,
    )


def solution(mesh):
    placed = (
        P("ctx", "tp", None),
        P("ctx", "tp", None),
        P("ctx", "tp", None),
        P("tp", None, None),
        P("tp", None),
        P("ctx", "tp", None),
    )
    return jax.shard_map(
        on_device,
        mesh=mesh,
        in_specs=placed,
        out_specs=(
            P("ctx", "tp", None),
            P("ctx", "tp", None),
            P("ctx", "tp", None),
            P("ctx", "tp", None),
            P("tp", None, None),
            P("tp", None),
        ),
        check_vma=False,
    )
```

time: 846 us -> 173 us (0.20)
  waiting for transfers between devices: 505 us -> 83.3 us
  other arithmetic: 136 us -> 0 us
  blocking collectives: 164 us -> 49.2 us
  starting transfers between devices: 0.08 us -> 25.1 us
  between operations: 13.9 us -> 0.73 us
  matrix products: 9.54 us -> 0 us
  Pallas kernels: 0 us -> 9 us
    all_gather x2 -> x0, waiting for transfers between devices: 384 us -> none  [carried_in(): everything = lax.all_gather(array, axis)]
    psum x3 -> x0, blocking collectives: 164 us -> none  [the longest x1 137 us: on_device(): d_state, d_gain = lax.psum((own_grad, gain_term), 'ctx')]
    select_n x128 -> x0, other arithmetic: 133 us -> none  [step(): return jnp.where(reached, new, before)]
    psum x1 -> x0, waiting for transfers between devices: 119 us -> none  [on_device(): d_state, d_gain = lax.psum((own_grad, gain_term), 'ctx')]
    all_to_all x0 -> x4, waiting for transfers between devices: none -> 83.3 us  [the longest x1 28.6 us: on_device(): after = lax.all_to_all(after, 'ctx', 0, 0)]
    all_to_all x0 -> x2, blocking collectives: none -> 49.2 us  [the longest x1 39.8 us: on_device(): gathered = lax.all_to_all(own.reshape(chunks), 'ctx', 0, 0)]
    all_to_all x0 -> x4, starting transfers between devices: none -> 25.1 us  [the longest x1 7.11 us: on_device(): after = lax.all_to_all(after, 'ctx', 0, 0)]
    dot_general x12 -> x0, matrix products: 9.54 us -> none  [the longest x1 1.93 us: on_device(): jnp.einsum('bjhd,bjhe->bhde', key_b, value_b, preferred_element_type=jnp....]
  transfers between devices with their start and end apart: 3 -> 4, of which waited for: 3 -> 4; matrix products, arithmetic and copies ran while one was open for 1% -> 0% of each run, Pallas kernels for 0% -> 3%
where the time goes in v1:
time: 173 us; the launch traced here: 172 us
  waiting for transfers between devices  83.3 us (48%)
  blocking collectives  49.2 us (28%)
  starting transfers between devices  25.1 us (15%)
  Pallas kernels  9 us (5%)
  local copies, waits for them, and re-layouts  4.88 us (3%)
    all_to_all x1, blocking collectives, on_device(): gathered = lax.all_to_all(own.reshape(chunks), 'ctx', 0, 0)  39.8 us
    all_to_all x1, waiting for transfers between devices, on_device(): after = lax.all_to_all(after, 'ctx', 0, 0)  28.6 us
    all_to_all x1, waiting for transfers between devices, on_device(): gathered = lax.all_to_all(grad.reshape(chunks), 'ctx', 0, 0)  20.7 us
    all_to_all x1, waiting for transfers between devices, on_device(): before = lax.all_to_all(before, 'ctx', 0, 0).reshape(states)  19.6 us
    all_to_all x1, waiting for transfers between devices, on_device(): term = lax.all_to_all(term, 'ctx', 0, 0)  14.4 us
    all_to_all x1, blocking collectives, on_device(): stats = lax.all_to_all(stats, 'tp', 0, 0)  9.45 us
    pallas_call x11, Pallas kernels, call(): pl.pallas_call(kernel, name=name, out_shape=outs, in_specs=[pl.BlockSpec(...  9 us
    all_to_all x1, starting transfers between devices, on_device(): after = lax.all_to_all(after, 'ctx', 0, 0)  7.11 us
  transfers between devices with their start and end apart: 4, of which 4 were waited for; matrix products, arithmetic and copies ran while one was open for 0% of the time, Pallas kernels for 3%

profile of v1, /device:TPU:24, one launch (start us, length us, event | category | flops | bytes accessed | tf_op | source)
XLA Modules:
  0.0 172.2 jit_solution(15312911860317757807)
XLA Ops:
  0.6 0.9 copy-done.2
  1.6 0.9 copy-done.3
  2.5 0.3 state.1
  2.9 39.8 %all_to_all.30.x_ref = f32[64,8,128]{2,1,0:T(8,128)S(1)} all-to-all(f32[64,8,128]{2,1,0:T(8,128)S(1)} %bitcast.19), channel_id=1, replica_groups=mesh['ctx'=64,'tp'=8] {'ctx'}, dimensions={0} | all-to-all | bytes 524288 | tf_op jit(solution)/shard_map/all_to_all | solution.py:217
  42.7 0.8 prefix.1
  43.4 6.1 %all-to-all-start.1 = ((f32[64,8,128]{2,1,0:T(8,128)}), f32[64,8,128]{2,1,0:T(8,128)S(1)}, u32[]{:S(2)}, u32[]{:S(2)}) async-start(f32[64,8,128]{2,1,0:T(8,128)} %prefix.1), calls=%async_computation.1 | async-start | bytes 524288 | tf_op jit(solution)/shard_map/all_to_all | solution.py:228
  49.5 0.7 local.1
  50.6 19.6 %all-to-all-done.1 = f32[64,8,128]{2,1,0:T(8,128)S(1)} async-done(((f32[64,8,128]{2,1,0:T(8,128)}), f32[64,8,128]{2,1,0:T(8,128)S(1)}, u32[]{:S(2)}, u32[]{:S(2)}) %all-to-all-start.1) | async-done | bytes 262176 | tf_op jit(solution)/shard_map/all_to_all | solution.py:228
  70.2 0.9 copy-done.4
  71.1 0.4 attn.1
  71.5 9.5 %all_to_all.31.stats_ref = f32[8,4,128]{2,1,0:T(4,128)S(1)} all-to-all(f32[8,4,128]{2,1,0:T(4,128)S(1)} %get-tuple-element.37), channel_id=1, replica_groups=mesh['ctx'=64,'tp'=8] {'tp'}, dimensions={0} | all-to-all | bytes 32768 | tf_op jit(solution)/shard_map/all_to_all | solution.py:238
  81.0 1.1 grad.1
  82.1 5.9 %all-to-all-start.3 = ((f32[64,8,128]{2,1,0:T(8,128)}), f32[64,8,128]{2,1,0:T(8,128)S(1)}, u32[]{:S(2)}, u32[]{:S(2)}) async-start(f32[64,8,128]{2,1,0:T(8,128)} %bitcast.7), calls=%async_computation.3 | async-start | bytes 524288 | tf_op jit(solution)/shard_map/all_to_all | solution.py:247
  88.0 0.9 normed.1
  88.9 20.7 %all-to-all-done.3.x_ref = f32[64,8,128]{2,1,0:T(8,128)S(1)} async-done(((f32[64,8,128]{2,1,0:T(8,128)}), f32[64,8,128]{2,1,0:T(8,128)S(1)}, u32[]{:S(2)}, u32[]{:S(2)}) %all-to-all-start.3) | async-done | bytes 262176 | tf_op jit(solution)/shard_map/all_to_all | solution.py:247
  109.6 6.0 %all-to-all-start.5 = ((f32[64,4,128]{2,1,0:T(4,128)}), f32[64,4,128]{2,1,0:T(4,128)S(1)}, u32[]{:S(2)}, u32[]{:S(2)}) async-start(f32[64,4,128]{2,1,0:T(4,128)} %get-tuple-element.51), calls=%async_computation.5 | async-start | bytes 262144 | tf_op jit(solution)/shard_map/all_to_all | solution.py:255
  115.6 0.9 suffix.1
  116.5 14.4 %all-to-all-done.5.x_ref = f32[64,4,128]{2,1,0:T(4,128)S(1)} async-done(((f32[64,4,128]{2,1,0:T(4,128)}), f32[64,4,128]{2,1,0:T(4,128)S(1)}, u32[]{:S(2)}, u32[]{:S(2)}) %all-to-all-start.5) | async-done | bytes 131104 | tf_op jit(solution)/shard_map/all_to_all | solution.py:255
  130.9 7.1 %all-to-all-start.4 = ((f32[64,16,128]{2,1,0:T(8,128)}), f32[64,16,128]{2,1,0:T(8,128)}, u32[]{:S(2)}, u32[]{:S(2)}) async-start(f32[64,16,128]{2,1,0:T(8,128)} %suffix.1), calls=%async_computation.4 | async-start | bytes 1048576 | tf_op jit(solution)/shard_map/all_to_all | solution.py:258
  138.0 0.6 gain_sum.1
  138.6 2.0 %back.1 = (bf16[1024,128]{1,0:T(8,128)(2,1)}, f32[4,256,128]{2,1,0:T(8,128)S(1)}, f32[4,256,128]{2,1,0:T(8,128)S(1)}) custom-call(bf16[4,256,128]{2,1,0:T(8,128)(2,1)S(1)} %get-tuple-element.42.dh_ref, bf16[4,256,128]{2,1,0:T(8,128)(2,1)S(1)} %get-tuple-element.32.vh_ref, bf16[4,256,128]{2,1,0:T(8,128)(2,1)S(1)} %get-tuple-element.31.kh_ref, ...), custom_call_target="tpu_custom_call" | custom-call | flops 335544320 | bytes 3145728 | tf_op jit(solution)/shard_map/back/pallas_call | solution.py:178
  140.6 28.6 %all-to-all-done.4 = f32[64,16,128]{2,1,0:T(8,128)} async-done(((f32[64,16,128]{2,1,0:T(8,128)}), f32[64,16,128]{2,1,0:T(8,128)}, u32[]{:S(2)}, u32[]{:S(2)}) %all-to-all-start.4) | async-done | bytes 524320 | tf_op jit(solution)/shard_map/all_to_all | solution.py:258
  169.2 1.8 %fusion = (f32[64,8,128]{2,1,0:T(8,128)}, f32[64,8,128]{2,1,0:T(8,128)S(1)}) fusion(f32[64,16,128]{2,1,0:T(8,128)} %all-to-all-done.4), kind=kLoop, calls=%fused_computation | loop fusion | bytes 1048576 | tf_op jit(solution)/shard_map/slice | solution.py:267
  171.0 1.3 last.1
  (10 shorter events, 0.4 us)
Async XLA Ops:
  0.6 1.0 copy-start.2
  1.6 0.9 copy-start.3
  43.4 6.1 %copy-start = (bf16[256,4,128]{2,1,0:T(4,128)(2,1)S(1)}, bf16[256,4,128]{2,1,0:T(4,128)(2,1)}, u32[]{:S(2)}) copy-start(bf16[256,4,128]{2,1,0:T(4,128)(2,1)} %param.6) | copy-start | bytes 786436
  43.4 26.7 %all-to-all-start.1 = ((f32[64,8,128]{2,1,0:T(8,128)}), f32[64,8,128]{2,1,0:T(8,128)S(1)}, u32[]{:S(2)}, u32[]{:S(2)}) async-start(f32[64,8,128]{2,1,0:T(8,128)} %prefix.1), calls=%async_computation.1 | async-start | bytes 524288 | tf_op jit(solution)/shard_map/all_to_all | solution.py:228
  49.5 1.0 copy-start.1
  49.5 0.9 copy-start.5
  70.2 1.0 copy-start.4
  82.1 27.6 %all-to-all-start.3 = ((f32[64,8,128]{2,1,0:T(8,128)}), f32[64,8,128]{2,1,0:T(8,128)S(1)}, u32[]{:S(2)}, u32[]{:S(2)}) async-start(f32[64,8,128]{2,1,0:T(8,128)} %bitcast.7), calls=%async_computation.3 | async-start | bytes 524288 | tf_op jit(solution)/shard_map/all_to_all | solution.py:247
  109.6 21.3 %all-to-all-start.5 = ((f32[64,4,128]{2,1,0:T(4,128)}), f32[64,4,128]{2,1,0:T(4,128)S(1)}, u32[]{:S(2)}, u32[]{:S(2)}) async-start(f32[64,4,128]{2,1,0:T(4,128)} %get-tuple-element.51), calls=%async_computation.5 | async-start | bytes 262144 | tf_op jit(solution)/shard_map/all_to_all | solution.py:255
  130.9 38.3 %all-to-all-start.4 = ((f32[64,16,128]{2,1,0:T(8,128)}), f32[64,16,128]{2,1,0:T(8,128)}, u32[]{:S(2)}, u32[]{:S(2)}) async-start(f32[64,16,128]{2,1,0:T(8,128)} %suffix.1), calls=%async_computation.4 | async-start | bytes 1048576 | tf_op jit(solution)/shard_map/all_to_all | solution.py:258

commit v2 on v1

--- a/solution.py
+++ b/solution.py
@@ -52,8 +52,9 @@
         vh_ref[h] = v
 
 
-def local_kernel(q_ref, kh_ref, vh_ref, qh_ref, scores_ref, attn_ref, q32):
+def local_kernel(q_ref, kh_ref, vh_ref, init_in, qh_ref, scores_ref, attn_ref, init_ref, q32):
     heads, tokens, _ = kh_ref.shape
+    init_ref[...] = init_in[...]
     q32[...] = q_ref[...].astype(F32)
     keep = causal(tokens)
     for h in range(heads):
@@ -71,22 +72,48 @@
         ch_ref[h] = c32[head_rows(h, tokens, heads), :]
 
 
-def prefix_kernel(x_ref, out_ref):
-    peers = x_ref.shape[0]
+def near_prefix_kernel(x_ref, pre_ref, total_ref):
+    members, rows = x_ref.shape[:2]
     total = jnp.zeros(x_ref.shape[1:], F32)
-    for i in range(peers):
-        out_ref[i] = total
+    for i in range(members):
+        pre_ref[i] = total
         total = total + x_ref[i]
-
-
-def suffix_kernel(x_ref, out_ref):
-    peers, rows = x_ref.shape[:2]
+    for g in range(total_ref.shape[0]):
+        total_ref[g] = total
+
+
+def far_prefix_kernel(totals_ref, pre_ref, out_ref):
+    groups, (members, rows, width) = totals_ref.shape[0], pre_ref.shape
+    own = lax.axis_index("ctx") // members
+    far = jnp.zeros((rows, width), F32)
+    for g in range(groups):
+        far = far + jnp.where(g < own, totals_ref[g], 0.0)
+    for i in range(members):
+        out_ref[i] = far + pre_ref[i]
+
+
+def near_suffix_kernel(x_ref, suf_ref, total_ref):
+    members, rows = suf_ref.shape[:2]
     total = jnp.zeros(x_ref.shape[1:], F32)
-    for i in reversed(range(peers)):
-        out_ref[i, :rows] = total
+    for i in reversed(range(members)):
+        suf_ref[i] = total[:rows]
         total = total + x_ref[i]
-    for i in range(peers):
-        out_ref[i, rows:] = total
+    for g in range(total_ref.shape[0]):
+        total_ref[g] = total
+
+
+def far_suffix_kernel(totals_ref, suf_ref, out_ref, gain_ref):
+    groups, (members, rows, width) = totals_ref.shape[0], suf_ref.shape
+    own = lax.axis_index("ctx") // members
+    far = jnp.zeros((rows, width), F32)
+    total = jnp.zeros(totals_ref.shape[1:], F32)
+    for g in range(groups):
+        total = total + totals_ref[g]
+        far = far + jnp.where(g > own, totals_ref[g, :rows], 0.0)
+    for i in range(members):
+        out_ref[i, :rows] = far + suf_ref[i]
+        out_ref[i, rows:] = total[:rows]
+    gain_ref[...] = total[rows : rows + gain_ref.shape[0]]
 
 
 def attn_kernel(before_ref, init_ref, qh_ref, local_ref, ch_ref, gain_ref, attn_ref, state_ref, stats_ref):
@@ -112,6 +139,9 @@
 
 def grad_kernel(width_total, stats_ref, attn_ref, ch_ref, gain_ref, qh_ref, dh_ref, grad_ref, scale_ref):
     heads, tokens, width = qh_ref.shape
+    members, padded, _ = grad_ref.shape
+    parts = members // heads
+    chunk = width // parts
     rows = stats_ref[0]
     for i in range(1, stats_ref.shape[0]):
         rows = rows + stats_ref[i]
@@ -122,25 +152,28 @@
     rscale = jnp.broadcast_to(rscale, (width, tokens)).T
     pull = jnp.broadcast_to(pull, (width, tokens)).T
     scale_ref[...] = rscale
+    terms = []
     for h in range(heads):
         gain = gain_ref[h : h + 1, :]
-        d_attn = (rscale * gain * ch_ref[h] - attn_ref[h] * pull).astype(BF16)
+        attn = attn_ref[h]
+        pushed = ch_ref[h] * rscale
+        d_attn = (gain * pushed - attn * pull).astype(BF16)
         dh_ref[h] = d_attn
-        grad_ref[h] = dot(qh_ref[h], d_attn, TN)
-
-
-def gain_kernel(attn_ref, ch_ref, gain_ref, scale_ref, normed_ref, term_ref, out32):
-    heads, tokens, _ = ch_ref.shape
+        grad = dot(qh_ref[h], d_attn, TN)
+        for p in range(parts):
+            grad_ref[h * parts + p, :chunk] = grad[p * chunk : (p + 1) * chunk]
+        terms.append(jnp.sum(pushed * attn, axis=0, keepdims=True))
+    terms = jnp.concatenate(terms + [jnp.zeros((padded - chunk - heads, width), F32)], axis=0)
+    for i in range(members):
+        grad_ref[i, chunk:] = terms
+
+
+def normed_kernel(attn_ref, gain_ref, scale_ref, normed_ref, out32):
+    heads, tokens, _ = attn_ref.shape
     rscale = scale_ref[...]
-    terms = []
-    for h in range(heads):
-        scaled = attn_ref[h] * rscale
-        out32[head_rows(h, tokens, heads), :] = scaled * gain_ref[h : h + 1, :]
-        terms.append(jnp.sum(ch_ref[h] * scaled, axis=0, keepdims=True))
+    for h in range(heads):
+        out32[head_rows(h, tokens, heads), :] = attn_ref[h] * rscale * gain_ref[h : h + 1, :]
     normed_ref[...] = out32[...].astype(BF16)
-    term = jnp.concatenate(terms, axis=0)
-    for i in range(term_ref.shape[0]):
-        term_ref[i] = term
 
 
 def back_kernel(dh_ref, vh_ref, kh_ref, qh_ref, state_ref, scores_ref, dq_ref, dk_ref, dv_ref, out32):
@@ -156,21 +189,19 @@
     dq_ref[...] = out32[...].astype(BF16)
 
 
-def last_kernel(after_ref, kh_ref, vh_ref, dk_in, dv_in, dk_ref, dv_ref, k32, v32):
-    heads, tokens, _ = kh_ref.shape
-    for h in range(heads):
-        after = after_ref[h]
+def last_kernel(after_ref, kh_ref, vh_ref, dk_in, dv_in, dk_ref, dv_ref, d_state_ref, k32, v32):
+    heads, tokens, width = kh_ref.shape
+    parts = after_ref.shape[0] // heads
+    chunk = width // parts
+    for h in range(heads):
+        pieces = [after_ref[h * parts + p, :chunk] for p in range(parts)]
+        after = jnp.concatenate(pieces, axis=0)
         k32[head_rows(h, tokens, heads), :] = dk_in[h] + times(vh_ref[h], after, True)
         v32[head_rows(h, tokens, heads), :] = dv_in[h] + times(kh_ref[h], after, False)
+        for p in range(parts):
+            d_state_ref[h, p * chunk : (p + 1) * chunk] = after_ref[h * parts + p, chunk:]
     dk_ref[...] = k32[...].astype(BF16)
     dv_ref[...] = v32[...].astype(BF16)
-
-
-def sum_kernel(x_ref, out_ref):
-    total = x_ref[0]
-    for i in range(1, x_ref.shape[0]):
-        total = total + x_ref[i]
-    out_ref[...] = total
 
 
 def call(kernel, name, outs, args, scratch=(), flops=0):
@@ -195,16 +226,24 @@
     tokens, heads, width = queries.shape
     peers = lax.axis_size("ctx")
     sharers = lax.axis_size("tp")
+    groups = 4
+    members = peers // groups
+    near = [[g * members + i for i in range(members)] for g in range(groups)]
+    far = [[g * members + i for g in range(groups)] for i in range(members)]
     width_total = heads * sharers * width
     flat = (tokens * heads, width)
     by_head = (heads, tokens, width)
     states = (heads, width, width)
-    chunk = heads * width // peers
-    chunks = (peers, chunk, width)
+    chunk = heads * width // members
+    chunks = (members, chunk, width)
+    padded = chunk + 8
     squares = (heads, tokens, tokens)
     wide = pltpu.VMEM(flat, F32)
     unit = 2 * tokens * width * width * heads
     q, k, v, c = (a.reshape(flat) for a in (queries, keys, values, cotangent))
+
+    def swap(x, lists):
+        return lax.all_to_all(x, "ctx", 0, 0, axis_index_groups=lists)
 
     own, kh, vh = call(
         state_kernel,
@@ -214,24 +253,27 @@
         [wide, wide],
         unit,
     )
-    gathered = lax.all_to_all(own.reshape(chunks), "ctx", 0, 0)
-    qh, scores, local = call(
+    gathered = swap(own.reshape(chunks), near)
+    qh, scores, local, init = call(
         local_kernel,
         "local",
-        [shape(by_head, BF16), shape(squares, BF16), shape(by_head)],
-        [q, kh, vh],
+        [shape(by_head, BF16), shape(squares, BF16), shape(by_head), shape(states)],
+        [q, kh, vh, init_state],
         [wide],
         4 * unit,
     )
-    (before,) = call(prefix_kernel, "prefix", [shape(chunks)], [gathered])
-    c, before = lax.optimization_barrier((c, before))
-    before = lax.all_to_all(before, "ctx", 0, 0).reshape(states)
+    pre, totals = call(
+        near_prefix_kernel, "near_prefix", [shape(chunks), shape((groups, chunk, width))], [gathered]
+    )
+    totals = swap(totals, far)
     (ch,) = call(cot_kernel, "cotangent", [shape(by_head)], [c, gain], [wide])
+    (before,) = call(far_prefix_kernel, "far_prefix", [shape(chunks)], [totals, pre])
+    before = swap(before, near).reshape(states)
     attn, state, stats = call(
         attn_kernel,
         "attn",
         [shape(by_head), shape(states), shape((sharers, 4, tokens // 2))],
-        [before, init_state, qh, local, ch, gain],
+        [before, init, qh, local, ch, gain],
         (),
         2 * unit,
     )
@@ -239,23 +281,17 @@
     dh, grad, scale = call(
         functools.partial(grad_kernel, width_total),
         "grad",
-        [shape(by_head, BF16), shape(states), shape((tokens, width))],
+        [shape(by_head, BF16), shape((members, padded, width)), shape((tokens, width))],
         [stats, attn, ch, gain, qh],
         (),
         unit,
     )
-    gathered = lax.all_to_all(grad.reshape(chunks), "ctx", 0, 0)
-    normed, term = call(
-        gain_kernel,
-        "normed",
-        [shape(flat, BF16), shape((peers, heads, width))],
-        [attn, ch, gain, scale],
-        [wide],
-    )
-    term = lax.all_to_all(term, "ctx", 0, 0)
-    (after,) = call(suffix_kernel, "suffix", [shape((peers, 2 * chunk, width))], [gathered])
-    dh, after = lax.optimization_barrier((dh, after))
-    after = lax.all_to_all(after, "ctx", 0, 0)
+    gathered = swap(grad, near)
+    (normed,) = call(normed_kernel, "normed", [shape(flat, BF16)], [attn, gain, scale], [wide])
+    suf, totals = call(
+        near_suffix_kernel, "near_suffix", [shape(chunks), shape((groups, padded, width))], [gathered]
+    )
+    totals = swap(totals, far)
     d_query, dk, dv = call(
         back_kernel,
         "back",
@@ -264,17 +300,21 @@
         [wide],
         10 * unit,
     )
-    d_state = after[:, chunk:].reshape(states)
-    after = after[:, :chunk].reshape(states)
-    d_key, d_value = call(
+    after, d_gain = call(
+        far_suffix_kernel,
+        "far_suffix",
+        [shape((members, 2 * chunk, width)), shape((heads, width))],
+        [totals, suf],
+    )
+    after = swap(after, near)
+    d_key, d_value, d_state = call(
         last_kernel,
         "last",
-        [shape(flat, BF16), shape(flat, BF16)],
+        [shape(flat, BF16), shape(flat, BF16), shape(states)],
         [after, kh, vh, dk, dv],
         [wide, wide],
         4 * unit,
     )
-    (d_gain,) = call(sum_kernel, "gain_sum", [shape((heads, width))], [term])
     whole = (tokens, heads, width)
     return (
         normed.reshape(whole),

time: 173 us -> 123 us (0.71)
  waiting for transfers between devices: 83.3 us -> 12.2 us
  blocking collectives: 49.2 us -> 82.8 us
  starting transfers between devices: 25.1 us -> 13 us
    all_to_all x4 -> x2, waiting for transfers between devices: 83.3 us -> 12.2 us  [swap(): return lax.all_to_all(x, 'ctx', 0, 0, axis_index_groups=lists)]
    all_to_all x1 -> x4, blocking collectives: 39.8 us -> 73.4 us  [swap(): return lax.all_to_all(x, 'ctx', 0, 0, axis_index_groups=lists)]
    all_to_all x4 -> x2, starting transfers between devices: 25.1 us -> 13 us  [swap(): return lax.all_to_all(x, 'ctx', 0, 0, axis_index_groups=lists)]
    slice x1 -> x0, local copies, waits for them, and re-layouts: 1.77 us -> none  [on_device(): d_state = after[:, chunk:].reshape(states)]
    unnamed x12 -> x16, local copies, waits for them, and re-layouts: 3.12 us -> 4.48 us
    pallas_call x11 -> x12, Pallas kernels: 9 us -> 7.69 us  [call(): pl.pallas_call(kernel, name=name, out_shape=outs, in_specs=[pl.BlockSpec(...]
  transfers between devices with their start and end apart: 4 -> 2, of which waited for: 4 -> 2; matrix products, arithmetic and copies ran while one was open for 0% -> 0% of each run, Pallas kernels for 3% -> 3%
where the time goes in v2:
time: 123 us; the launch traced here: 121 us
  blocking collectives  82.8 us (67%)
  starting transfers between devices  13 us (11%)
  waiting for transfers between devices  12.2 us (10%)
  Pallas kernels  7.69 us (6%)
  local copies, waits for them, and re-layouts  4.48 us (4%)
    all_to_all x4, blocking collectives, swap(): return lax.all_to_all(x, 'ctx', 0, 0, axis_index_groups=lists)  73.4 us
    all_to_all x2, starting transfers between devices, swap(): return lax.all_to_all(x, 'ctx', 0, 0, axis_index_groups=lists)  13 us
    all_to_all x2, waiting for transfers between devices, swap(): return lax.all_to_all(x, 'ctx', 0, 0, axis_index_groups=lists)  12.2 us
    all_to_all x1, blocking collectives, on_device(): stats = lax.all_to_all(stats, 'tp', 0, 0)  9.45 us
    pallas_call x12, Pallas kernels, call(): pl.pallas_call(kernel, name=name, out_shape=outs, in_specs=[pl.BlockSpec(...  7.69 us
    unnamed x16, local copies, waits for them, and re-layouts  4.48 us
  transfers between devices with their start and end apart: 2, of which 2 were waited for; matrix products, arithmetic and copies ran while one was open for 0% of the time, Pallas kernels for 3%

profile of v2, /device:TPU:24, one launch (start us, length us, event | category | flops | bytes accessed | tf_op | source)
XLA Modules:
  0.0 120.9 jit_solution(7469930320407800996)
XLA Ops:
  0.6 0.9 copy-done.1
  1.6 0.9 copy-done.2
  2.5 0.3 state.1
  2.9 16.8 %all_to_all.35.x_ref = f32[16,32,128]{2,1,0:T(8,128)S(1)} all-to-all(f32[16,32,128]{2,1,0:T(8,128)S(1)} %bitcast.14), channel_id=1, replica_groups={{0,8,16,24,32,40,48,56,64,72,80,88,96,104,112,120},{128,136,144,152,160..., dimensions={0} | all-to-all | bytes 524288 | tf_op jit(solution)/shard_map/all_to_all | solution.py:246
  19.7 25.2 %all_to_all.36.totals_ref = f32[4,32,128]{2,1,0:T(8,128)S(1)} all-to-all(f32[4,32,128]{2,1,0:T(8,128)S(1)} %get-tuple-element.32), channel_id=1, replica_groups={{0,128,256,384},{8,136,264,392},{16,144,272,400},{24,152,280,408},{32,1..., dimensions={0} | all-to-all | bytes 131072 | tf_op jit(solution)/shard_map/all_to_all | solution.py:246
  44.9 0.7 far_prefix.1
  45.7 6.3 %all-to-all-start.2 = ((f32[16,32,128]{2,1,0:T(8,128)}), f32[16,32,128]{2,1,0:T(8,128)S(1)}, u32[]{:S(2)}, u32[]{:S(2)}) async-start(f32[16,32,128]{2,1,0:T(8,128)} %far_prefix.1), calls=%async_computation.2 | async-start | bytes 524288 | tf_op jit(solution)/shard_map/all_to_all | solution.py:246
  52.0 0.1 cotangent.1.ch_ref
  52.1 0.8 copy-done.3
  53.1 0.7 local.1
  53.8 0.7 copy-done.5
  54.4 4.1 %all-to-all-done.2 = f32[16,32,128]{2,1,0:T(8,128)S(1)} async-done(((f32[16,32,128]{2,1,0:T(8,128)}), f32[16,32,128]{2,1,0:T(8,128)S(1)}, u32[]{:S(2)}, u32[]{:S(2)}) %all-to-all-start.2) | async-done | bytes 262176 | tf_op jit(solution)/shard_map/all_to_all | solution.py:246
  58.5 0.9 copy-done.6
  59.5 0.4 attn.1
  59.9 9.5 %all_to_all.37.stats_ref = f32[8,4,128]{2,1,0:T(4,128)S(1)} all-to-all(f32[8,4,128]{2,1,0:T(4,128)S(1)} %get-tuple-element.40), channel_id=1, replica_groups=mesh['ctx'=64,'tp'=8] {'tp'}, dimensions={0} | all-to-all | bytes 32768 | tf_op jit(solution)/shard_map/all_to_all | solution.py:280
  69.4 0.4 grad.1
  69.8 15.8 %all_to_all.38.x_ref = f32[16,40,128]{2,1,0:T(8,128)S(1)} all-to-all(f32[16,40,128]{2,1,0:T(8,128)S(1)} %get-tuple-element.46), channel_id=1, replica_groups={{0,8,16,24,32,40,48,56,64,72,80,88,96,104,112,120},{128,136,144,152,160..., dimensions={0} | all-to-all | bytes 655360 | tf_op jit(solution)/shard_map/all_to_all | solution.py:246
  85.7 15.5 %all_to_all.39.totals_ref = f32[4,40,128]{2,1,0:T(8,128)S(1)} all-to-all(f32[4,40,128]{2,1,0:T(8,128)S(1)} %get-tuple-element.47), channel_id=1, replica_groups={{0,128,256,384},{8,136,264,392},{16,144,272,400},{24,152,280,408},{32,1..., dimensions={0} | all-to-all | bytes 163840 | tf_op jit(solution)/shard_map/all_to_all | solution.py:246
  101.2 0.8 far_suffix.1
  102.0 6.7 %all-to-all-start.6 = ((f32[16,64,128]{2,1,0:T(8,128)}), f32[16,64,128]{2,1,0:T(8,128)S(1)}, u32[]{:S(2)}, u32[]{:S(2)}) async-start(f32[16,64,128]{2,1,0:T(8,128)} %get-tuple-element.49), calls=%async_computation.6 | async-start | bytes 1048576 | tf_op jit(solution)/shard_map/all_to_all | solution.py:246
  108.7 0.8 normed.1
  109.5 2.0 %back.1 = (bf16[1024,128]{1,0:T(8,128)(2,1)}, f32[4,256,128]{2,1,0:T(8,128)S(1)}, f32[4,256,128]{2,1,0:T(8,128)S(1)}) custom-call(bf16[4,256,128]{2,1,0:T(8,128)(2,1)S(1)} %get-tuple-element.42.dh_ref, bf16[4,256,128]{2,1,0:T(8,128)(2,1)S(1)} %get-tuple-element.35.vh_ref, bf16[4,256,128]{2,1,0:T(8,128)(2,1)S(1)} %get-tuple-element.34.kh_ref, ...), custom_call_target="tpu_custom_call" | custom-call | flops 335544320 | bytes 3145728 | tf_op jit(solution)/shard_map/back/pallas_call | solution.py:209
  111.5 8.1 %all-to-all-done.6.after_ref = f32[16,64,128]{2,1,0:T(8,128)S(1)} async-done(((f32[16,64,128]{2,1,0:T(8,128)}), f32[16,64,128]{2,1,0:T(8,128)S(1)}, u32[]{:S(2)}, u32[]{:S(2)}) %all-to-all-start.6) | async-done | bytes 524320 | tf_op jit(solution)/shard_map/all_to_all | solution.py:246
  119.6 1.3 %last.1 = (bf16[1024,128]{1,0:T(8,128)(2,1)}, bf16[1024,128]{1,0:T(8,128)(2,1)}, f32[4,128,128]{2,1,0:T(8,128)}) custom-call(f32[16,64,128]{2,1,0:T(8,128)S(1)} %all-to-all-done.6.after_ref, bf16[4,256,128]{2,1,0:T(8,128)(2,1)S(1)} %get-tuple-element.34.kh_ref, bf16[4,256,128]{2,1,0:T(8,128)(2,1)S(1)} %get-tuple-element.35.vh_ref, ...), custom_call_target="tpu_custom_call" | custom-call | flops 134217728 | bytes 2883584 | tf_op jit(solution)/shard_map/last/pallas_call | solution.py:209
  (13 shorter events, 0.2 us)
Async XLA Ops:
  0.6 1.0 copy-start.1
  1.6 0.9 copy-start.2
  45.7 6.3 %copy-start = (bf16[256,4,128]{2,1,0:T(4,128)(2,1)S(1)}, bf16[256,4,128]{2,1,0:T(4,128)(2,1)}, u32[]{:S(2)}) copy-start(bf16[256,4,128]{2,1,0:T(4,128)(2,1)} %param.11) | copy-start | bytes 786436
  45.7 6.3 %copy-start.7 = (f32[4,128]{1,0:T(4,128)S(1)}, f32[4,128]{1,0:T(4,128)}, u32[]{:S(2)}) copy-start(f32[4,128]{1,0:T(4,128)} %gain_ref.7) | copy-start | bytes 6148
  45.7 12.9 %all-to-all-start.2 = ((f32[16,32,128]{2,1,0:T(8,128)}), f32[16,32,128]{2,1,0:T(8,128)S(1)}, u32[]{:S(2)}, u32[]{:S(2)}) async-start(f32[16,32,128]{2,1,0:T(8,128)} %far_prefix.1), calls=%async_computation.2 | async-start | bytes 524288 | tf_op jit(solution)/shard_map/all_to_all | solution.py:246
  52.0 1.0 copy-start.3
  52.0 1.0 copy-start.4
  53.7 0.7 copy-start.5
  58.5 1.0 copy-start.6
  102.0 17.5 %all-to-all-start.6 = ((f32[16,64,128]{2,1,0:T(8,128)}), f32[16,64,128]{2,1,0:T(8,128)S(1)}, u32[]{:S(2)}, u32[]{:S(2)}) async-start(f32[16,64,128]{2,1,0:T(8,128)} %get-tuple-element.49), calls=%async_computation.6 | async-start | bytes 1048576 | tf_op jit(solution)/shard_map/all_to_all | solution.py:246

commit v3 on v2

--- a/solution.py
+++ b/solution.py
@@ -15,6 +15,19 @@
 TN = (((0,), (0,)), ((), ()))
 
 
+def led_by(first, count):
+    return (first,) + tuple(i for i in range(count) if i != first)
+
+
+OUT1, BACK1 = led_by(10, 16), led_by(6, 16)
+OUT2, BACK2 = led_by(6, 16), led_by(10, 16)
+FAR1, FAR2 = (2, 0, 3, 1), (2, 0, 3, 1)
+
+
+def found(out, back):
+    return tuple(back.index(member) for member in out)
+
+
 def dot(a, b, dims):
     return lax.dot_general(a, b, dims, preferred_element_type=F32)
 
@@ -40,10 +53,16 @@
     return rows >= cols
 
 
-def state_kernel(k_ref, v_ref, state_ref, kh_ref, vh_ref, k32, v32):
+def state_kernel(k_hbm, v_hbm, state_ref, kh_ref, vh_ref, k_in, v_in, k32, v32, sems):
     heads, tokens, _ = kh_ref.shape
-    k32[...] = k_ref[...].astype(F32)
-    v32[...] = v_ref[...].astype(F32)
+    k_copy = pltpu.make_async_copy(k_hbm, k_in, sems.at[0])
+    v_copy = pltpu.make_async_copy(v_hbm, v_in, sems.at[1])
+    k_copy.start()
+    v_copy.start()
+    k_copy.wait()
+    k32[...] = k_in[...].astype(F32)
+    v_copy.wait()
+    v32[...] = v_in[...].astype(F32)
     for h in range(heads):
         k = k32[head_rows(h, tokens, heads), :].astype(BF16)
         v = v32[head_rows(h, tokens, heads), :].astype(BF16)
@@ -52,9 +71,12 @@
         vh_ref[h] = v
 
 
-def local_kernel(q_ref, kh_ref, vh_ref, init_in, qh_ref, scores_ref, attn_ref, init_ref, q32):
+def local_kernel(
+    q_ref, kh_ref, vh_ref, init_in, gain_in, qh_ref, scores_ref, attn_ref, init_ref, gain_ref, q32
+):
     heads, tokens, _ = kh_ref.shape
     init_ref[...] = init_in[...]
+    gain_ref[...] = gain_in[...]
     q32[...] = q_ref[...].astype(F32)
     keep = causal(tokens)
     for h in range(heads):
@@ -65,11 +87,11 @@
         attn_ref[h] = dot(scores, vh_ref[h], NN)
 
 
-def cot_kernel(c_ref, gain_ref, ch_ref, c32):
+def cot_kernel(c_ref, ch_ref, c32):
     heads, tokens, _ = ch_ref.shape
     c32[...] = c_ref[...].astype(F32)
     for h in range(heads):
-        ch_ref[h] = c32[head_rows(h, tokens, heads), :]
+        ch_ref[h] = c32[head_rows(h, tokens, heads), :].astype(BF16)
 
 
 def near_prefix_kernel(x_ref, pre_ref, total_ref):
@@ -77,7 +99,7 @@
     total = jnp.zeros(x_ref.shape[1:], F32)
     for i in range(members):
         pre_ref[i] = total
-        total = total + x_ref[i]
+        total = total + x_ref[OUT1.index(i)]
     for g in range(total_ref.shape[0]):
         total_ref[g] = total
 
@@ -87,9 +109,9 @@
     own = lax.axis_index("ctx") // members
     far = jnp.zeros((rows, width), F32)
     for g in range(groups):
-        far = far + jnp.where(g < own, totals_ref[g], 0.0)
-    for i in range(members):
-        out_ref[i] = far + pre_ref[i]
+        far = far + jnp.where(FAR1[g] < own, totals_ref[g], 0.0)
+    for j in range(members):
+        out_ref[j] = far + pre_ref[BACK1[j]]
 
 
 def near_suffix_kernel(x_ref, suf_ref, total_ref):
@@ -97,36 +119,38 @@
     total = jnp.zeros(x_ref.shape[1:], F32)
     for i in reversed(range(members)):
         suf_ref[i] = total[:rows]
-        total = total + x_ref[i]
+        total = total + x_ref[OUT2.index(i)]
     for g in range(total_ref.shape[0]):
         total_ref[g] = total
 
 
-def far_suffix_kernel(totals_ref, suf_ref, out_ref, gain_ref):
+def far_suffix_kernel(totals_ref, suf_ref, out_ref):
     groups, (members, rows, width) = totals_ref.shape[0], suf_ref.shape
     own = lax.axis_index("ctx") // members
     far = jnp.zeros((rows, width), F32)
-    total = jnp.zeros(totals_ref.shape[1:], F32)
+    total = jnp.zeros((rows, width), F32)
     for g in range(groups):
-        total = total + totals_ref[g]
-        far = far + jnp.where(g > own, totals_ref[g, :rows], 0.0)
-    for i in range(members):
-        out_ref[i, :rows] = far + suf_ref[i]
-        out_ref[i, rows:] = total[:rows]
-    gain_ref[...] = total[rows : rows + gain_ref.shape[0]]
+        total = total + totals_ref[g, :rows]
+        far = far + jnp.where(FAR2[g] > own, totals_ref[g, :rows], 0.0)
+    for j in range(members):
+        out_ref[j, :rows] = far + suf_ref[BACK2[j]]
+        out_ref[j, rows:] = total
 
 
 def attn_kernel(before_ref, init_ref, qh_ref, local_ref, ch_ref, gain_ref, attn_ref, state_ref, stats_ref):
     heads, tokens, width = qh_ref.shape
+    parts = before_ref.shape[0] // heads
+    places = found(OUT1, BACK1)
     ssq = jnp.zeros((tokens, width), F32)
     gdot = jnp.zeros((tokens, width), F32)
     for h in range(heads):
-        state = init_ref[h] + before_ref[h]
+        pieces = [before_ref[j] for j in places[h * parts : (h + 1) * parts]]
+        state = init_ref[h] + jnp.concatenate(pieces, axis=0)
         state_ref[h] = state
         attn = local_ref[h] + times(qh_ref[h], state, False)
         attn_ref[h] = attn
         ssq = ssq + attn * attn
-        gdot = gdot + gain_ref[h : h + 1, :] * ch_ref[h] * attn
+        gdot = gdot + gain_ref[h : h + 1, :] * ch_ref[h].astype(F32) * attn
     ssq_row = jnp.sum(ssq.T, axis=0, keepdims=True)
     gdot_row = jnp.sum(gdot.T, axis=0, keepdims=True)
     half = tokens // 2
@@ -156,7 +180,7 @@
     for h in range(heads):
         gain = gain_ref[h : h + 1, :]
         attn = attn_ref[h]
-        pushed = ch_ref[h] * rscale
+        pushed = ch_ref[h].astype(F32) * rscale
         d_attn = (gain * pushed - attn * pull).astype(BF16)
         dh_ref[h] = d_attn
         grad = dot(qh_ref[h], d_attn, TN)
@@ -189,31 +213,55 @@
     dq_ref[...] = out32[...].astype(BF16)
 
 
-def last_kernel(after_ref, kh_ref, vh_ref, dk_in, dv_in, dk_ref, dv_ref, d_state_ref, k32, v32):
+def last_kernel(
+    after_ref, totals_ref, kh_ref, vh_ref, dk_in, dv_in,
+    dk_hbm, dv_hbm, state_hbm, gain_hbm, k32, v32, dk, dv, states, gain, sems,
+):
     heads, tokens, width = kh_ref.shape
     parts = after_ref.shape[0] // heads
     chunk = width // parts
-    for h in range(heads):
-        pieces = [after_ref[h * parts + p, :chunk] for p in range(parts)]
+    places = found(OUT2, BACK2)
+    for h in range(heads):
+        for p in range(parts):
+            states[h, p * chunk : (p + 1) * chunk] = after_ref[places[h * parts + p], chunk:]
+    state_copy = pltpu.make_async_copy(states, state_hbm, sems.at[0])
+    state_copy.start()
+    total = totals_ref[0, chunk:]
+    for g in range(1, totals_ref.shape[0]):
+        total = total + totals_ref[g, chunk:]
+    gain[...] = total[:heads]
+    gain_copy = pltpu.make_async_copy(gain, gain_hbm, sems.at[3])
+    gain_copy.start()
+    afters = []
+    for h in range(heads):
+        pieces = [after_ref[j, :chunk] for j in places[h * parts : (h + 1) * parts]]
         after = jnp.concatenate(pieces, axis=0)
+        afters.append(after)
         k32[head_rows(h, tokens, heads), :] = dk_in[h] + times(vh_ref[h], after, True)
-        v32[head_rows(h, tokens, heads), :] = dv_in[h] + times(kh_ref[h], after, False)
-        for p in range(parts):
-            d_state_ref[h, p * chunk : (p + 1) * chunk] = after_ref[h * parts + p, chunk:]
-    dk_ref[...] = k32[...].astype(BF16)
-    dv_ref[...] = v32[...].astype(BF16)
-
-
-def call(kernel, name, outs, args, scratch=(), flops=0):
+    dk[...] = k32[...].astype(BF16)
+    dk_copy = pltpu.make_async_copy(dk, dk_hbm, sems.at[1])
+    dk_copy.start()
+    for h in range(heads):
+        v32[head_rows(h, tokens, heads), :] = dv_in[h] + times(kh_ref[h], afters[h], False)
+    dv[...] = v32[...].astype(BF16)
+    dv_copy = pltpu.make_async_copy(dv, dv_hbm, sems.at[2])
+    dv_copy.start()
+    state_copy.wait()
+    gain_copy.wait()
+    dk_copy.wait()
+    dv_copy.wait()
+
+
+def call(kernel, name, outs, args, scratch=(), flops=0, places=(pltpu.VMEM, pltpu.VMEM), limit=24):
     moved = sum(a.size * a.dtype.itemsize for a in list(args) + list(outs))
     return pl.pallas_call(
         kernel,
         name=name,
         out_shape=outs,
-        in_specs=[pl.BlockSpec(memory_space=pltpu.VMEM)] * len(args),
-        out_specs=[pl.BlockSpec(memory_space=pltpu.VMEM)] * len(outs),
+        in_specs=[pl.BlockSpec(memory_space=places[0])] * len(args),
+        out_specs=[pl.BlockSpec(memory_space=places[1])] * len(outs),
         scratch_shapes=scratch,
-        compiler_params=pltpu.CompilerParams(vmem_limit_bytes=24 * 2**20),
+        compiler_params=pltpu.CompilerParams(vmem_limit_bytes=limit * 2**20),
         cost_estimate=pl.CostEstimate(flops=flops, bytes_accessed=moved, transcendentals=0),
     )(*args)
 
@@ -228,8 +276,12 @@
     sharers = lax.axis_size("tp")
     groups = 4
     members = peers // groups
-    near = [[g * members + i for i in range(members)] for g in range(groups)]
-    far = [[g * members + i for g in range(groups)] for i in range(members)]
+    def near(order):
+        return [[g * members + i for i in order] for g in range(groups)]
+
+    def far(order):
+        return [[g * members + i for g in order] for i in range(members)]
+
     width_total = heads * sharers * width
     flat = (tokens * heads, width)
     by_head = (heads, tokens, width)
@@ -239,6 +291,7 @@
     padded = chunk + 8
     squares = (heads, tokens, tokens)
     wide = pltpu.VMEM(flat, F32)
+    half = pltpu.VMEM(flat, BF16)
     unit = 2 * tokens * width * width * heads
     q, k, v, c = (a.reshape(flat) for a in (queries, keys, values, cotangent))
 
@@ -249,26 +302,28 @@
         state_kernel,
         "state",
         [shape(states), shape(by_head, BF16), shape(by_head, BF16)],
-        [k, v],
-        [wide, wide],
+        [pltpu.with_memory_space_constraint(k, pltpu.HBM), pltpu.with_memory_space_constraint(v, pltpu.HBM)],
+        [half, half, wide, wide, pltpu.SemaphoreType.DMA((2,))],
         unit,
-    )
-    gathered = swap(own.reshape(chunks), near)
-    qh, scores, local, init = call(
+        (pltpu.HBM, pltpu.VMEM),
+    )
+    gathered = swap(own.reshape(chunks), near(OUT1))
+    pre, totals = call(
+        near_prefix_kernel, "near_prefix", [shape(chunks), shape((groups, chunk, width))], [gathered]
+    )
+    totals = swap(totals, far(FAR1))
+    totals, q, c, init_state = lax.optimization_barrier((totals, q, c, init_state))
+    qh, scores, local, init, gain = call(
         local_kernel,
         "local",
-        [shape(by_head, BF16), shape(squares, BF16), shape(by_head), shape(states)],
-        [q, kh, vh, init_state],
+        [shape(by_head, BF16), shape(squares, BF16), shape(by_head), shape(states), shape((heads, width))],
+        [q, kh, vh, init_state, gain],
         [wide],
         4 * unit,
     )
-    pre, totals = call(
-        near_prefix_kernel, "near_prefix", [shape(chunks), shape((groups, chunk, width))], [gathered]
-    )
-    totals = swap(totals, far)
-    (ch,) = call(cot_kernel, "cotangent", [shape(by_head)], [c, gain], [wide])
+    (ch,) = call(cot_kernel, "cotangent", [shape(by_head, BF16)], [c], [wide])
     (before,) = call(far_prefix_kernel, "far_prefix", [shape(chunks)], [totals, pre])
-    before = swap(before, near).reshape(states)
+    before = swap(before, near(BACK1))
     attn, state, stats = call(
         attn_kernel,
         "attn",
@@ -286,12 +341,11 @@
         (),
         unit,
     )
-    gathered = swap(grad, near)
+    gathered = swap(grad, near(OUT2))
     (normed,) = call(normed_kernel, "normed", [shape(flat, BF16)], [attn, gain, scale], [wide])
     suf, totals = call(
         near_suffix_kernel, "near_suffix", [shape(chunks), shape((groups, padded, width))], [gathered]
     )
-    totals = swap(totals, far)
     d_query, dk, dv = call(
         back_kernel,
         "back",
@@ -300,20 +354,28 @@
         [wide],
         10 * unit,
     )
-    after, d_gain = call(
-        far_suffix_kernel,
-        "far_suffix",
-        [shape((members, 2 * chunk, width)), shape((heads, width))],
-        [totals, suf],
-    )
-    after = swap(after, near)
-    d_key, d_value, d_state = call(
+    totals, normed, d_query, dk, dv = lax.optimization_barrier((totals, normed, d_query, dk, dv))
+    totals = swap(totals, far(FAR2))
+    (after,) = call(
+        far_suffix_kernel, "far_suffix", [shape((members, 2 * chunk, width))], [totals, suf]
+    )
+    after = swap(after, near(BACK2))
+    d_key, d_value, d_state, d_gain = call(
         last_kernel,
         "last",
-        [shape(flat, BF16), shape(flat, BF16), shape(states)],
-        [after, kh, vh, dk, dv],
-        [wide, wide],
+        [shape(flat, BF16), shape(flat, BF16), shape(states), shape((heads, width))],
+        [after, totals, kh, vh, dk, dv],
+        [
+            wide,
+            wide,
+            half,
+            half,
+            pltpu.VMEM(states, F32),
+            pltpu.VMEM((heads, width), F32),
+            pltpu.SemaphoreType.DMA((4,)),
+        ],
         4 * unit,
+        (pltpu.VMEM, pltpu.HBM),
     )
     whole = (tokens, heads, width)
     return (

time: 123 us -> 108 us (0.88); the launches traced: 121 us -> 108 us
  blocking collectives: 82.8 us -> 74.8 us
  local copies, waits for them, and re-layouts: 4.48 us -> 0.95 us
  starting transfers between devices: 13 us -> 9.85 us
    all_to_all x4, blocking collectives: 73.4 us -> 65.3 us  [swap(): return lax.all_to_all(x, 'ctx', 0, 0, axis_index_groups=lists)]
    unnamed x16 -> x8, local copies, waits for them, and re-layouts: 4.48 us -> 0.95 us
    all_to_all x2, starting transfers between devices: 13 us -> 9.85 us  [swap(): return lax.all_to_all(x, 'ctx', 0, 0, axis_index_groups=lists)]
where the time goes in v3:
time: 108 us
  blocking collectives  74.8 us (69%)
  waiting for transfers between devices  12.8 us (12%)
  starting transfers between devices  9.85 us (9%)
  Pallas kernels  8.61 us (8%)
    all_to_all x4, blocking collectives, swap(): return lax.all_to_all(x, 'ctx', 0, 0, axis_index_groups=lists)  65.3 us
    all_to_all x2, waiting for transfers between devices, swap(): return lax.all_to_all(x, 'ctx', 0, 0, axis_index_groups=lists)  12.8 us
    all_to_all x2, starting transfers between devices, swap(): return lax.all_to_all(x, 'ctx', 0, 0, axis_index_groups=lists)  9.85 us
    all_to_all x1, blocking collectives, on_device(): stats = lax.all_to_all(stats, 'tp', 0, 0)  9.45 us
    pallas_call x12, Pallas kernels, call(): pl.pallas_call(kernel, name=name, out_shape=outs, in_specs=[pl.BlockSpec(...  8.61 us
  transfers between devices with their start and end apart: 2, of which 2 were waited for; matrix products, arithmetic and copies ran while one was open for 0% of the time, Pallas kernels for 3%

profile of v3, /device:TPU:24, one launch (start us, length us, event | category | flops | bytes accessed | tf_op | source)
XLA Modules:
  0.0 107.7 jit_solution(7267011690843032230)
XLA Ops:
  0.6 1.4 %state.1 = (f32[4,128,128]{2,1,0:T(8,128)S(1)}, bf16[4,256,128]{2,1,0:T(8,128)(2,1)S(1)}, bf16[4,256,128]{2,1,0:T(8,128)(2,1)S(1)}) custom-call(bf16[1024,128]{1,0:T(8,128)(2,1)} %bitcast.13, bf16[1024,128]{1,0:T(8,128)(2,1)} %bitcast.14), custom_call_target="tpu_custom_call" | custom-call | flops 33554432 | bytes 1310720 | tf_op jit(solution)/shard_map/state/pallas_call | solution.py:257
  2.0 15.7 %all_to_all.35.x_ref = f32[16,32,128]{2,1,0:T(8,128)S(1)} all-to-all(f32[16,32,128]{2,1,0:T(8,128)S(1)} %bitcast.10), channel_id=1, replica_groups={{80,0,8,16,24,32,40,48,56,64,72,88,96,104,112,120},{208,128,136,144,152..., dimensions={0} | all-to-all | bytes 524288 | tf_op jit(solution)/shard_map/all_to_all | solution.py:299
  17.7 17.4 %all_to_all.36.totals_ref = f32[4,32,128]{2,1,0:T(8,128)S(1)} all-to-all(f32[4,32,128]{2,1,0:T(8,128)S(1)} %get-tuple-element.41), channel_id=1, replica_groups={{256,0,384,128},{264,8,392,136},{272,16,400,144},{280,24,408,152},{288,..., dimensions={0} | all-to-all | bytes 131072 | tf_op jit(solution)/shard_map/all_to_all | solution.py:299
  35.1 0.7 far_prefix.1
  35.9 5.2 %all-to-all-start.2 = ((f32[16,32,128]{2,1,0:T(8,128)}), f32[16,32,128]{2,1,0:T(8,128)S(1)}, u32[]{:S(2)}, u32[]{:S(2)}) async-start(f32[16,32,128]{2,1,0:T(8,128)} %far_prefix.1), calls=%async_computation.2 | async-start | bytes 524288 | tf_op jit(solution)/shard_map/all_to_all | solution.py:299
  41.0 0.0 copy-done
  41.0 0.0 copy-start.1
  41.1 0.0 copy-start.2
  41.1 0.1 cotangent.1.ch_ref
  41.1 0.0 copy-start.3
  41.2 0.8 copy-done.1
  42.0 0.1 copy-done.2
  42.1 0.7 local.1
  42.8 5.5 %all-to-all-done.2.before_ref = f32[16,32,128]{2,1,0:T(8,128)S(1)} async-done(((f32[16,32,128]{2,1,0:T(8,128)}), f32[16,32,128]{2,1,0:T(8,128)S(1)}, u32[]{:S(2)}, u32[]{:S(2)}) %all-to-all-start.2) | async-done | bytes 262176 | tf_op jit(solution)/shard_map/all_to_all | solution.py:299
  48.3 0.4 attn.1
  48.7 9.5 %all_to_all.37.stats_ref = f32[8,4,128]{2,1,0:T(4,128)S(1)} all-to-all(f32[8,4,128]{2,1,0:T(4,128)S(1)} %get-tuple-element.53), channel_id=1, replica_groups=mesh['ctx'=64,'tp'=8] {'tp'}, dimensions={0} | all-to-all | bytes 32768 | tf_op jit(solution)/shard_map/all_to_all | solution.py:335
  58.1 1.1 %grad.1 = (bf16[4,256,128]{2,1,0:T(8,128)(2,1)S(1)}, f32[16,40,128]{2,1,0:T(8,128)}, f32[256,128]{1,0:T(8,128)S(1)}) custom-call(f32[8,4,128]{2,1,0:T(4,128)S(1)} %all_to_all.37.stats_ref, f32[4,256,128]{2,1,0:T(8,128)S(1)} %get-tuple-element.54.attn_ref, bf16[4,256,128]{2,1,0:T(8,128)(2,1)S(1)} %cotangent.1.ch_ref, ...), custom_call_target="tpu_custom_call" | custom-call | flops 33554432 | bytes 1787904 | tf_op jit(solution)/shard_map/grad/pallas_call | solution.py:257
  59.3 4.7 %all-to-all-start.4 = ((f32[16,40,128]{2,1,0:T(8,128)}), f32[16,40,128]{2,1,0:T(8,128)S(1)}, u32[]{:S(2)}, u32[]{:S(2)}) async-start(f32[16,40,128]{2,1,0:T(8,128)} %get-tuple-element.55), calls=%async_computation.4 | async-start | bytes 655360 | tf_op jit(solution)/shard_map/all_to_all | solution.py:299
  64.0 0.8 normed.1
  64.8 2.0 %back.1 = (bf16[1024,128]{1,0:T(8,128)(2,1)}, f32[4,256,128]{2,1,0:T(8,128)S(1)}, f32[4,256,128]{2,1,0:T(8,128)S(1)}) custom-call(bf16[4,256,128]{2,1,0:T(8,128)(2,1)S(1)} %get-tuple-element.58.dh_ref, bf16[4,256,128]{2,1,0:T(8,128)(2,1)S(1)} %get-tuple-element.46.vh_ref, bf16[4,256,128]{2,1,0:T(8,128)(2,1)S(1)} %get-tuple-element.45.kh_ref, ...), custom_call_target="tpu_custom_call" | custom-call | flops 335544320 | bytes 3145728 | tf_op jit(solution)/shard_map/back/pallas_call | solution.py:257
  66.8 7.3 %all-to-all-done.4.x_ref = f32[16,40,128]{2,1,0:T(8,128)S(1)} async-done(((f32[16,40,128]{2,1,0:T(8,128)}), f32[16,40,128]{2,1,0:T(8,128)S(1)}, u32[]{:S(2)}, u32[]{:S(2)}) %all-to-all-start.4) | async-done | bytes 327712 | tf_op jit(solution)/shard_map/all_to_all | solution.py:299
  74.1 16.6 %all_to_all.38.totals_ref = f32[4,40,128]{2,1,0:T(8,128)S(1)} all-to-all(f32[4,40,128]{2,1,0:T(8,128)S(1)} %get-tuple-element.66), channel_id=1, replica_groups={{256,0,384,128},{264,8,392,136},{272,16,400,144},{280,24,408,152},{288,..., dimensions={0} | all-to-all | bytes 163840 | tf_op jit(solution)/shard_map/all_to_all | solution.py:299
  90.7 15.6 %all_to_all.39.after_ref = f32[16,64,128]{2,1,0:T(8,128)S(1)} all-to-all(f32[16,64,128]{2,1,0:T(8,128)S(1)} %far_suffix.1), channel_id=1, replica_groups={{80,0,8,16,24,32,40,48,56,64,72,88,96,104,112,120},{208,128,136,144,152..., dimensions={0} | all-to-all | bytes 1048576 | tf_op jit(solution)/shard_map/all_to_all | solution.py:299
  106.3 1.4 %last.1 = (bf16[1024,128]{1,0:T(8,128)(2,1)}, bf16[1024,128]{1,0:T(8,128)(2,1)}, f32[4,128,128]{2,1,0:T(8,128)}, f32[4,128]{1,0:T(4,128)}) custom-call(f32[16,64,128]{2,1,0:T(8,128)S(1)} %all_to_all.39.after_ref, f32[4,40,128]{2,1,0:T(8,128)S(1)} %all_to_all.38.totals_ref, bf16[4,256,128]{2,1,0:T(8,128)(2,1)S(1)} %get-tuple-element.45.kh_ref, ...), custom_call_target="tpu_custom_call" | custom-call | flops 134217728 | bytes 2967552 | tf_op jit(solution)/shard_map/last/pallas_call | solution.py:257
  (5 shorter events, 0.1 us)
Async XLA Ops:
  35.9 5.2 %copy-start = (bf16[256,4,128]{2,1,0:T(4,128)(2,1)S(1)}, bf16[256,4,128]{2,1,0:T(4,128)(2,1)}, u32[]{:S(2)}) copy-start(bf16[256,4,128]{2,1,0:T(4,128)(2,1)} %param.11) | copy-start | bytes 786436
  35.9 12.4 %all-to-all-start.2 = ((f32[16,32,128]{2,1,0:T(8,128)}), f32[16,32,128]{2,1,0:T(8,128)S(1)}, u32[]{:S(2)}, u32[]{:S(2)}) async-start(f32[16,32,128]{2,1,0:T(8,128)} %far_prefix.1), calls=%async_computation.2 | async-start | bytes 524288 | tf_op jit(solution)/shard_map/all_to_all | solution.py:299
  41.0 1.0 copy-start.1
  41.1 1.0 copy-start.2
  41.1 0.9 copy-start.3
  59.3 14.8 %all-to-all-start.4 = ((f32[16,40,128]{2,1,0:T(8,128)}), f32[16,40,128]{2,1,0:T(8,128)S(1)}, u32[]{:S(2)}, u32[]{:S(2)}) async-start(f32[16,40,128]{2,1,0:T(8,128)} %get-tuple-element.55), calls=%async_computation.4 | async-start | bytes 655360 | tf_op jit(solution)/shard_map/all_to_all | solution.py:299

commit v4 on v3

--- a/solution.py
+++ b/solution.py
@@ -16,12 +16,12 @@
 
 
 def led_by(first, count):
-    return (first,) + tuple(i for i in range(count) if i != first)
+    return [first] + [i for i in range(count) if i != first]
 
 
 OUT1, BACK1 = led_by(10, 16), led_by(6, 16)
 OUT2, BACK2 = led_by(6, 16), led_by(10, 16)
-FAR1, FAR2 = (2, 0, 3, 1), (2, 0, 3, 1)
+FAR1, FAR2 = [2, 0, 3, 1], [2, 0, 3, 1]
 
 
 def found(out, back):
@@ -37,14 +37,17 @@
     return high, (a - high.astype(F32)).astype(BF16)
 
 
-def times(a, m, turned):
-    high, low = split(m)
-    both = jnp.concatenate([high, low], axis=1 if turned else 0)
+def times(a, parts, turned):
+    both = jnp.concatenate(parts, axis=1 if turned else 0)
     return dot(jnp.concatenate([a, a], axis=1), both, NT if turned else NN)
 
 
 def head_rows(h, tokens, heads):
     return pl.ds(h, tokens, stride=heads)
+
+
+def masked(a, b, keep):
+    return jnp.where(keep, dot(a, b, NT), 0.0).astype(BF16)
 
 
 def causal(tokens):
@@ -72,7 +75,7 @@
 
 
 def local_kernel(
-    q_ref, kh_ref, vh_ref, init_in, gain_in, qh_ref, scores_ref, attn_ref, init_ref, gain_ref, q32
+    q_ref, kh_ref, vh_ref, init_in, gain_in, qh_ref, attn_ref, init_ref, gain_ref, q32
 ):
     heads, tokens, _ = kh_ref.shape
     init_ref[...] = init_in[...]
@@ -82,9 +85,7 @@
     for h in range(heads):
         q = q32[head_rows(h, tokens, heads), :].astype(BF16)
         qh_ref[h] = q
-        scores = jnp.where(keep, dot(q, kh_ref[h], NT), 0.0).astype(BF16)
-        scores_ref[h] = scores
-        attn_ref[h] = dot(scores, vh_ref[h], NN)
+        attn_ref[h] = dot(masked(q, kh_ref[h], keep), vh_ref[h], NN)
 
 
 def cot_kernel(c_ref, ch_ref, c32):
@@ -147,7 +148,7 @@
         pieces = [before_ref[j] for j in places[h * parts : (h + 1) * parts]]
         state = init_ref[h] + jnp.concatenate(pieces, axis=0)
         state_ref[h] = state
-        attn = local_ref[h] + times(qh_ref[h], state, False)
+        attn = local_ref[h] + times(qh_ref[h], split(state), False)
         attn_ref[h] = attn
         ssq = ssq + attn * attn
         gdot = gdot + gain_ref[h : h + 1, :] * ch_ref[h].astype(F32) * attn
@@ -161,7 +162,50 @@
         stats_ref[i] = rows
 
 
-def grad_kernel(width_total, stats_ref, attn_ref, ch_ref, gain_ref, qh_ref, dh_ref, grad_ref, scale_ref):
+def query_grad(dh_ref, kh_ref, vh_ref, state_ref, dq_ref, out32):
+    heads, tokens, _ = kh_ref.shape
+    keep = causal(tokens)
+    for h in range(heads):
+        d_attn = dh_ref[h]
+        back = masked(d_attn, vh_ref[h], keep)
+        d_query = dot(back, kh_ref[h], NN) + times(d_attn, split(state_ref[h]), True)
+        out32[head_rows(h, tokens, heads), :] = d_query
+    dq_ref[...] = out32[...].astype(BF16)
+
+
+def down(row, width):
+    return jnp.broadcast_to(row, (width, row.shape[1])).T
+
+
+def normed_rows(attn_ref, gain_ref, scale_ref, normed_ref, out32):
+    heads, tokens, width = attn_ref.shape
+    rscale = down(scale_ref[...], width)
+    for h in range(heads):
+        out32[head_rows(h, tokens, heads), :] = attn_ref[h] * rscale * gain_ref[h : h + 1, :]
+    normed_ref[...] = out32[...].astype(BF16)
+
+
+def finished_rows(
+    dh_ref, kh_ref, vh_ref, state_ref, attn_ref, gain_ref, scale_ref, dq_hbm, normed_hbm, dq, normed, wide, sems
+):
+    query_grad(dh_ref, kh_ref, vh_ref, state_ref, dq, wide)
+    dq_copy = pltpu.make_async_copy(dq, dq_hbm, sems.at[0])
+    dq_copy.start()
+    normed_rows(attn_ref, gain_ref, scale_ref, normed, wide)
+    normed_copy = pltpu.make_async_copy(normed, normed_hbm, sems.at[1])
+    normed_copy.start()
+    dq_copy.wait()
+    normed_copy.wait()
+
+
+def first_core():
+    return lax.axis_index("tp") % 2 == 0
+
+
+def grad_kernel(
+    width_total, stats_ref, attn_ref, ch_ref, gain_ref, qh_ref, kh_ref, vh_ref, state_ref,
+    dh_ref, grad_ref, scale_ref, dq_hbm, normed_hbm, dq, normed, wide, sems,
+):
     heads, tokens, width = qh_ref.shape
     members, padded, _ = grad_ref.shape
     parts = members // heads
@@ -173,9 +217,9 @@
     gdot = jnp.concatenate([rows[2:3], rows[3:4]], axis=1)
     rscale = lax.rsqrt(ssq / width_total + EPS)
     pull = rscale * rscale * rscale * gdot / width_total
-    rscale = jnp.broadcast_to(rscale, (width, tokens)).T
-    pull = jnp.broadcast_to(pull, (width, tokens)).T
     scale_ref[...] = rscale
+    rscale = down(rscale, width)
+    pull = down(pull, width)
     terms = []
     for h in range(heads):
         gain = gain_ref[h : h + 1, :]
@@ -191,26 +235,31 @@
     for i in range(members):
         grad_ref[i, chunk:] = terms
 
-
-def normed_kernel(attn_ref, gain_ref, scale_ref, normed_ref, out32):
-    heads, tokens, _ = attn_ref.shape
-    rscale = scale_ref[...]
-    for h in range(heads):
-        out32[head_rows(h, tokens, heads), :] = attn_ref[h] * rscale * gain_ref[h : h + 1, :]
-    normed_ref[...] = out32[...].astype(BF16)
-
-
-def back_kernel(dh_ref, vh_ref, kh_ref, qh_ref, state_ref, scores_ref, dq_ref, dk_ref, dv_ref, out32):
+    @pl.when(first_core())
+    def _():
+        finished_rows(
+            dh_ref, kh_ref, vh_ref, state_ref, attn_ref, gain_ref, scale_ref,
+            dq_hbm, normed_hbm, dq, normed, wide, sems,
+        )
+
+
+def back_kernel(
+    dh_ref, vh_ref, kh_ref, qh_ref, state_ref, attn_ref, gain_ref, scale_ref, dq_in, normed_in,
+    dq_hbm, normed_hbm, dk_ref, dv_ref, dq, normed, wide, sems,
+):
     heads, tokens, _ = kh_ref.shape
     keep = causal(tokens)
     for h in range(heads):
-        d_attn = dh_ref[h]
-        back = jnp.where(keep, dot(d_attn, vh_ref[h], NT), 0.0).astype(BF16)
-        d_query = dot(back, kh_ref[h], NN) + times(d_attn, state_ref[h], True)
-        out32[head_rows(h, tokens, heads), :] = d_query
-        dk_ref[h] = dot(back, qh_ref[h], TN)
-        dv_ref[h] = dot(scores_ref[h], d_attn, TN)
-    dq_ref[...] = out32[...].astype(BF16)
+        q, d_attn = qh_ref[h], dh_ref[h]
+        dk_ref[h] = dot(masked(d_attn, vh_ref[h], keep), q, TN)
+        dv_ref[h] = dot(masked(q, kh_ref[h], keep), d_attn, TN)
+
+    @pl.when(jnp.logical_not(first_core()))
+    def _():
+        finished_rows(
+            dh_ref, kh_ref, vh_ref, state_ref, attn_ref, gain_ref, scale_ref,
+            dq_hbm, normed_hbm, dq, normed, wide, sems,
+        )
 
 
 def last_kernel(
@@ -235,7 +284,7 @@
     afters = []
     for h in range(heads):
         pieces = [after_ref[j, :chunk] for j in places[h * parts : (h + 1) * parts]]
-        after = jnp.concatenate(pieces, axis=0)
+        after = split(jnp.concatenate(pieces, axis=0))
         afters.append(after)
         k32[head_rows(h, tokens, heads), :] = dk_in[h] + times(vh_ref[h], after, True)
     dk[...] = k32[...].astype(BF16)
@@ -252,16 +301,21 @@
     dv_copy.wait()
 
 
-def call(kernel, name, outs, args, scratch=(), flops=0, places=(pltpu.VMEM, pltpu.VMEM), limit=24):
+def call(kernel, name, outs, args, scratch=(), flops=0, hbm_args=(), hbm_outs=(), aliases={}):
     moved = sum(a.size * a.dtype.itemsize for a in list(args) + list(outs))
+
+    def places(count, hbm):
+        return [pl.BlockSpec(memory_space=pltpu.HBM if i in hbm else pltpu.VMEM) for i in range(count)]
+
     return pl.pallas_call(
         kernel,
         name=name,
         out_shape=outs,
-        in_specs=[pl.BlockSpec(memory_space=places[0])] * len(args),
-        out_specs=[pl.BlockSpec(memory_space=places[1])] * len(outs),
+        in_specs=places(len(args), hbm_args),
+        out_specs=places(len(outs), hbm_outs),
         scratch_shapes=scratch,
-        compiler_params=pltpu.CompilerParams(vmem_limit_bytes=limit * 2**20),
+        input_output_aliases=aliases,
+        compiler_params=pltpu.CompilerParams(vmem_limit_bytes=24 * 2**20),
         cost_estimate=pl.CostEstimate(flops=flops, bytes_accessed=moved, transcendentals=0),
     )(*args)
 
@@ -289,7 +343,6 @@
     chunk = heads * width // members
     chunks = (members, chunk, width)
     padded = chunk + 8
-    squares = (heads, tokens, tokens)
     wide = pltpu.VMEM(flat, F32)
     half = pltpu.VMEM(flat, BF16)
     unit = 2 * tokens * width * width * heads
@@ -302,10 +355,10 @@
         state_kernel,
         "state",
         [shape(states), shape(by_head, BF16), shape(by_head, BF16)],
-        [pltpu.with_memory_space_constraint(k, pltpu.HBM), pltpu.with_memory_space_constraint(v, pltpu.HBM)],
+        [pltpu.with_memory_space_constraint(a, pltpu.HBM) for a in (k, v)],
         [half, half, wide, wide, pltpu.SemaphoreType.DMA((2,))],
         unit,
-        (pltpu.HBM, pltpu.VMEM),
+        hbm_args=(0, 1),
     )
     gathered = swap(own.reshape(chunks), near(OUT1))
     pre, totals = call(
@@ -313,10 +366,10 @@
     )
     totals = swap(totals, far(FAR1))
     totals, q, c, init_state = lax.optimization_barrier((totals, q, c, init_state))
-    qh, scores, local, init, gain = call(
+    qh, local, init, gain = call(
         local_kernel,
         "local",
-        [shape(by_head, BF16), shape(squares, BF16), shape(by_head), shape(states), shape((heads, width))],
+        [shape(by_head, BF16), shape(by_head), shape(states), shape((heads, width))],
         [q, kh, vh, init_state, gain],
         [wide],
         4 * unit,
@@ -332,27 +385,36 @@
         (),
         2 * unit,
     )
-    stats = lax.all_to_all(stats, "tp", 0, 0)
-    dh, grad, scale = call(
+    stats = lax.all_to_all(stats, "tp", 0, 0, axis_index_groups=[led_by(5, sharers)])
+    dh, grad, scale, d_query, normed = call(
         functools.partial(grad_kernel, width_total),
         "grad",
-        [shape(by_head, BF16), shape((members, padded, width)), shape((tokens, width))],
-        [stats, attn, ch, gain, qh],
-        (),
-        unit,
+        [
+            shape(by_head, BF16),
+            shape((members, padded, width)),
+            shape((1, tokens)),
+            shape(flat, BF16),
+            shape(flat, BF16),
+        ],
+        [stats, attn, ch, gain, qh, kh, vh, state],
+        [half, half, wide, pltpu.SemaphoreType.DMA((2,))],
+        5 * unit,
+        hbm_outs=(3, 4),
     )
     gathered = swap(grad, near(OUT2))
-    (normed,) = call(normed_kernel, "normed", [shape(flat, BF16)], [attn, gain, scale], [wide])
     suf, totals = call(
         near_suffix_kernel, "near_suffix", [shape(chunks), shape((groups, padded, width))], [gathered]
     )
-    d_query, dk, dv = call(
+    d_query, normed, dk, dv = call(
         back_kernel,
         "back",
-        [shape(flat, BF16), shape(by_head), shape(by_head)],
-        [dh, vh, kh, qh, state, scores],
-        [wide],
+        [shape(flat, BF16), shape(flat, BF16), shape(by_head), shape(by_head)],
+        [dh, vh, kh, qh, state, attn, gain, scale, d_query, normed],
+        [half, half, wide, pltpu.SemaphoreType.DMA((2,))],
         10 * unit,
+        hbm_args=(8, 9),
+        hbm_outs=(0, 1),
+        aliases={8: 0, 9: 1},
     )
     totals, normed, d_query, dk, dv = lax.optimization_barrier((totals, normed, d_query, dk, dv))
     totals = swap(totals, far(FAR2))
@@ -375,7 +437,7 @@
             pltpu.SemaphoreType.DMA((4,)),
         ],
         4 * unit,
-        (pltpu.VMEM, pltpu.HBM),
+        hbm_outs=(0, 1, 2, 3),
     )
     whole = (tokens, heads, width)
     return (

time: 108 us -> 105 us (0.972)
  blocking collectives: 74.8 us -> 71.2 us
    all_to_all x1, blocking collectives: 9.45 us -> 7.34 us  [on_device(): lax.all_to_all(stats, 'tp', 0, 0, axis_index_groups=[led_by(5, sharers)])]
    all_to_all x4, blocking collectives: 65.3 us -> 63.9 us  [swap(): return lax.all_to_all(x, 'ctx', 0, 0, axis_index_groups=lists)]
    pallas_call x12 -> x11, Pallas kernels: 8.61 us -> 8.54 us  [call(): pl.pallas_call(kernel, name=name, out_shape=outs, in_specs=places(len(arg...]
  transfers between devices with their start and end apart: 2 -> 2, of which waited for: 2 -> 2; matrix products, arithmetic and copies ran while one was open for 0% -> 0% of each run, Pallas kernels for 3% -> 2%
where the time goes in v4:
time: 105 us
  blocking collectives  71.2 us (68%)
  waiting for transfers between devices  13.2 us (13%)
  starting transfers between devices  9.87 us (9%)
  Pallas kernels  8.54 us (8%)
    all_to_all x4, blocking collectives, swap(): return lax.all_to_all(x, 'ctx', 0, 0, axis_index_groups=lists)  63.9 us
    all_to_all x2, waiting for transfers between devices, swap(): return lax.all_to_all(x, 'ctx', 0, 0, axis_index_groups=lists)  13.2 us
    all_to_all x2, starting transfers between devices, swap(): return lax.all_to_all(x, 'ctx', 0, 0, axis_index_groups=lists)  9.87 us
    pallas_call x11, Pallas kernels, call(): pl.pallas_call(kernel, name=name, out_shape=outs, in_specs=places(len(arg...  8.54 us
    all_to_all x1, blocking collectives, on_device(): lax.all_to_all(stats, 'tp', 0, 0, axis_index_groups=[led_by(5, sharers)])  7.34 us
  transfers between devices with their start and end apart: 2, of which 2 were waited for; matrix products, arithmetic and copies ran while one was open for 0% of the time, Pallas kernels for 2%

profile of v4, /device:TPU:24, one launch (start us, length us, event | category | flops | bytes accessed | tf_op | source)
XLA Modules:
  0.0 104.5 jit_solution(2032492249516227527)
XLA Ops:
  0.6 1.4 %state.1 = (f32[4,128,128]{2,1,0:T(8,128)S(1)}, bf16[4,256,128]{2,1,0:T(8,128)(2,1)S(1)}, bf16[4,256,128]{2,1,0:T(8,128)(2,1)S(1)}) custom-call(bf16[1024,128]{1,0:T(8,128)(2,1)} %bitcast.14, bf16[1024,128]{1,0:T(8,128)(2,1)} %bitcast.15), custom_call_target="tpu_custom_call" | custom-call | flops 33554432 | bytes 1310720 | tf_op jit(solution)/shard_map/state/pallas_call | solution.py:310
  2.0 15.7 %all_to_all.35.x_ref = f32[16,32,128]{2,1,0:T(8,128)S(1)} all-to-all(f32[16,32,128]{2,1,0:T(8,128)S(1)} %bitcast.10), channel_id=1, replica_groups={{80,0,8,16,24,32,40,48,56,64,72,88,96,104,112,120},{208,128,136,144,152..., dimensions={0} | all-to-all | bytes 524288 | tf_op jit(solution)/shard_map/all_to_all | solution.py:352
  17.7 17.4 %all_to_all.36.totals_ref = f32[4,32,128]{2,1,0:T(8,128)S(1)} all-to-all(f32[4,32,128]{2,1,0:T(8,128)S(1)} %get-tuple-element.43), channel_id=1, replica_groups={{256,0,384,128},{264,8,392,136},{272,16,400,144},{280,24,408,152},{288,..., dimensions={0} | all-to-all | bytes 131072 | tf_op jit(solution)/shard_map/all_to_all | solution.py:352
  35.1 0.7 far_prefix.1
  35.9 5.2 %all-to-all-start.2 = ((f32[16,32,128]{2,1,0:T(8,128)}), f32[16,32,128]{2,1,0:T(8,128)S(1)}, u32[]{:S(2)}, u32[]{:S(2)}) async-start(f32[16,32,128]{2,1,0:T(8,128)} %far_prefix.1), calls=%async_computation.2 | async-start | bytes 524288 | tf_op jit(solution)/shard_map/all_to_all | solution.py:352
  41.0 0.0 copy-done
  41.0 0.0 copy-start.1
  41.1 0.0 copy-start.2
  41.1 0.1 cotangent.1.ch_ref
  41.1 0.0 copy-start.3
  41.2 0.8 copy-done.1
  42.0 0.1 copy-done.2
  42.1 0.0 copy-done.3
  42.1 0.7 local.1
  42.8 5.5 %all-to-all-done.2.before_ref = f32[16,32,128]{2,1,0:T(8,128)S(1)} async-done(((f32[16,32,128]{2,1,0:T(8,128)}), f32[16,32,128]{2,1,0:T(8,128)S(1)}, u32[]{:S(2)}, u32[]{:S(2)}) %all-to-all-start.2) | async-done | bytes 262176 | tf_op jit(solution)/shard_map/all_to_all | solution.py:352
  48.3 0.4 attn.1
  48.7 7.3 %all_to_all.37.stats_ref = f32[8,4,128]{2,1,0:T(4,128)S(1)} all-to-all(f32[8,4,128]{2,1,0:T(4,128)S(1)} %get-tuple-element.55), channel_id=1, replica_groups={{5,0,1,2,3,4,6,7},{13,8,9,10,11,12,14,15},{21,16,17,18,19,20,22,23},{29..., dimensions={0} | all-to-all | bytes 32768 | tf_op jit(solution)/shard_map/all_to_all | solution.py:388
  56.0 2.7 %grad.1 = (bf16[4,256,128]{2,1,0:T(8,128)(2,1)S(1)}, f32[16,40,128]{2,1,0:T(8,128)}, f32[1,256]{1,0:T(1,128)S(1)}, bf16[1024,128]{1,0:T(8,128)(2,1)}, bf16[1024,128]{1,0:T(8,128)(2,1)}) custom-call(f32[8,4,128]{2,1,0:T(4,128)S(1)} %all_to_all.37.stats_ref, f32[4,256,128]{2,1,0:T(8,128)S(1)} %get-tuple-element.56.attn_ref, ...), custom_call_target="tpu_custom_call" | custom-call | flops 167772160 | bytes 2968576 | tf_op jit(solution)/shard_map/grad/pallas_call | solution.py:310
  58.7 4.7 %all-to-all-start.4 = ((f32[16,40,128]{2,1,0:T(8,128)}), f32[16,40,128]{2,1,0:T(8,128)S(1)}, u32[]{:S(2)}, u32[]{:S(2)}) async-start(f32[16,40,128]{2,1,0:T(8,128)} %get-tuple-element.58), calls=%async_computation.4 | async-start | bytes 655360 | tf_op jit(solution)/shard_map/all_to_all | solution.py:352
  63.4 1.1 %back.1 = (bf16[1024,128]{1,0:T(8,128)(2,1)}, bf16[1024,128]{1,0:T(8,128)(2,1)}, f32[4,256,128]{2,1,0:T(8,128)S(1)}, f32[4,256,128]{2,1,0:T(8,128)S(1)}) custom-call(bf16[4,256,128]{2,1,0:T(8,128)(2,1)S(1)} %get-tuple-element.60.dh_ref, bf16[4,256,128]{2,1,0:T(8,128)(2,1)S(1)} %get-tuple-element.48.vh_ref, ...), custom_call_target="tpu_custom_call", output_to_operand_aliasing={{0}: (8, {}), {1}: (9, {})} | custom-call | flops 335544320 | bytes 3935232 | tf_op jit(solution)/shard_map/back/pallas_call | solution.py:310
  64.6 7.7 %all-to-all-done.4.x_ref = f32[16,40,128]{2,1,0:T(8,128)S(1)} async-done(((f32[16,40,128]{2,1,0:T(8,128)}), f32[16,40,128]{2,1,0:T(8,128)S(1)}, u32[]{:S(2)}, u32[]{:S(2)}) %all-to-all-start.4) | async-done | bytes 327712 | tf_op jit(solution)/shard_map/all_to_all | solution.py:352
  72.3 15.5 %all_to_all.38.totals_ref = f32[4,40,128]{2,1,0:T(8,128)S(1)} all-to-all(f32[4,40,128]{2,1,0:T(8,128)S(1)} %get-tuple-element.70), channel_id=1, replica_groups={{256,0,384,128},{264,8,392,136},{272,16,400,144},{280,24,408,152},{288,..., dimensions={0} | all-to-all | bytes 163840 | tf_op jit(solution)/shard_map/all_to_all | solution.py:352
  87.8 15.3 %all_to_all.39.after_ref = f32[16,64,128]{2,1,0:T(8,128)S(1)} all-to-all(f32[16,64,128]{2,1,0:T(8,128)S(1)} %far_suffix.1), channel_id=1, replica_groups={{80,0,8,16,24,32,40,48,56,64,72,88,96,104,112,120},{208,128,136,144,152..., dimensions={0} | all-to-all | bytes 1048576 | tf_op jit(solution)/shard_map/all_to_all | solution.py:352
  103.2 1.4 %last.1 = (bf16[1024,128]{1,0:T(8,128)(2,1)}, bf16[1024,128]{1,0:T(8,128)(2,1)}, f32[4,128,128]{2,1,0:T(8,128)}, f32[4,128]{1,0:T(4,128)}) custom-call(f32[16,64,128]{2,1,0:T(8,128)S(1)} %all_to_all.39.after_ref, f32[4,40,128]{2,1,0:T(8,128)S(1)} %all_to_all.38.totals_ref, bf16[4,256,128]{2,1,0:T(8,128)(2,1)S(1)} %get-tuple-element.47.kh_ref, ...), custom_call_target="tpu_custom_call" | custom-call | flops 134217728 | bytes 2967552 | tf_op jit(solution)/shard_map/last/pallas_call | solution.py:310
  (4 shorter events, 0.1 us)
Async XLA Ops:
  35.9 5.2 %copy-start = (bf16[256,4,128]{2,1,0:T(4,128)(2,1)S(1)}, bf16[256,4,128]{2,1,0:T(4,128)(2,1)}, u32[]{:S(2)}) copy-start(bf16[256,4,128]{2,1,0:T(4,128)(2,1)} %param.11) | copy-start | bytes 786436
  35.9 12.4 %all-to-all-start.2 = ((f32[16,32,128]{2,1,0:T(8,128)}), f32[16,32,128]{2,1,0:T(8,128)S(1)}, u32[]{:S(2)}, u32[]{:S(2)}) async-start(f32[16,32,128]{2,1,0:T(8,128)} %far_prefix.1), calls=%async_computation.2 | async-start | bytes 524288 | tf_op jit(solution)/shard_map/all_to_all | solution.py:352
  41.0 1.0 copy-start.1
  41.1 1.0 copy-start.2
  41.1 0.9 copy-start.3
  58.7 13.6 %all-to-all-start.4 = ((f32[16,40,128]{2,1,0:T(8,128)}), f32[16,40,128]{2,1,0:T(8,128)S(1)}, u32[]{:S(2)}, u32[]{:S(2)}) async-start(f32[16,40,128]{2,1,0:T(8,128)} %get-tuple-element.58), calls=%async_computation.4 | async-start | bytes 655360 | tf_op jit(solution)/shard_map/all_to_all | solution.py:352

commit v5 on v4

--- a/solution.py
+++ b/solution.py
@@ -116,13 +116,19 @@
 
 
 def near_suffix_kernel(x_ref, suf_ref, total_ref):
-    members, rows = suf_ref.shape[:2]
-    total = jnp.zeros(x_ref.shape[1:], F32)
+    members, rows, width = suf_ref.shape
+    slot = x_ref.shape[0] // members
+    total = jnp.zeros((rows, width), F32)
+    terms = jnp.zeros((slot - rows, width), F32)
     for i in reversed(range(members)):
-        suf_ref[i] = total[:rows]
-        total = total + x_ref[OUT2.index(i)]
+        first = OUT2.index(i) * slot
+        suf_ref[i] = total
+        total = total + x_ref[first : first + rows]
+        terms = terms + x_ref[first + rows : first + slot]
+    unused = jnp.zeros((total_ref.shape[1] - slot, width), F32)
     for g in range(total_ref.shape[0]):
-        total_ref[g] = total
+        total_ref[g, :rows] = total
+        total_ref[g, rows:] = jnp.concatenate([terms, unused], axis=0)
 
 
 def far_suffix_kernel(totals_ref, suf_ref, out_ref):
@@ -207,9 +213,9 @@
     dh_ref, grad_ref, scale_ref, dq_hbm, normed_hbm, dq, normed, wide, sems,
 ):
     heads, tokens, width = qh_ref.shape
-    members, padded, _ = grad_ref.shape
-    parts = members // heads
+    parts = (grad_ref.shape[0] - heads * width) // (heads * heads)
     chunk = width // parts
+    slot = chunk + heads
     rows = stats_ref[0]
     for i in range(1, stats_ref.shape[0]):
         rows = rows + stats_ref[i]
@@ -229,11 +235,12 @@
         dh_ref[h] = d_attn
         grad = dot(qh_ref[h], d_attn, TN)
         for p in range(parts):
-            grad_ref[h * parts + p, :chunk] = grad[p * chunk : (p + 1) * chunk]
+            first = (h * parts + p) * slot
+            grad_ref[first : first + chunk] = grad[p * chunk : (p + 1) * chunk]
         terms.append(jnp.sum(pushed * attn, axis=0, keepdims=True))
-    terms = jnp.concatenate(terms + [jnp.zeros((padded - chunk - heads, width), F32)], axis=0)
-    for i in range(members):
-        grad_ref[i, chunk:] = terms
+    terms = jnp.concatenate(terms, axis=0)
+    for i in range(heads * parts):
+        grad_ref[i * slot + chunk : (i + 1) * slot] = terms
 
     @pl.when(first_core())
     def _():
@@ -275,10 +282,10 @@
             states[h, p * chunk : (p + 1) * chunk] = after_ref[places[h * parts + p], chunk:]
     state_copy = pltpu.make_async_copy(states, state_hbm, sems.at[0])
     state_copy.start()
-    total = totals_ref[0, chunk:]
+    total = totals_ref[0, chunk : chunk + heads]
     for g in range(1, totals_ref.shape[0]):
-        total = total + totals_ref[g, chunk:]
-    gain[...] = total[:heads]
+        total = total + totals_ref[g, chunk : chunk + heads]
+    gain[...] = total
     gain_copy = pltpu.make_async_copy(gain, gain_hbm, sems.at[3])
     gain_copy.start()
     afters = []
@@ -361,11 +368,11 @@
         hbm_args=(0, 1),
     )
     gathered = swap(own.reshape(chunks), near(OUT1))
+    gathered, q, c, init_state = lax.optimization_barrier((gathered, q, c, init_state))
     pre, totals = call(
         near_prefix_kernel, "near_prefix", [shape(chunks), shape((groups, chunk, width))], [gathered]
     )
     totals = swap(totals, far(FAR1))
-    totals, q, c, init_state = lax.optimization_barrier((totals, q, c, init_state))
     qh, local, init, gain = call(
         local_kernel,
         "local",
@@ -375,6 +382,9 @@
         4 * unit,
     )
     (ch,) = call(cot_kernel, "cotangent", [shape(by_head, BF16)], [c], [wide])
+    totals, qh, local, init, gain, ch = lax.optimization_barrier(
+        (totals, qh, local, init, gain, ch)
+    )
     (before,) = call(far_prefix_kernel, "far_prefix", [shape(chunks)], [totals, pre])
     before = swap(before, near(BACK1))
     attn, state, stats = call(
@@ -391,7 +401,7 @@
         "grad",
         [
             shape(by_head, BF16),
-            shape((members, padded, width)),
+            shape((members * (chunk + heads), width)),
             shape((1, tokens)),
             shape(flat, BF16),
             shape(flat, BF16),
@@ -401,10 +411,18 @@
         5 * unit,
         hbm_outs=(3, 4),
     )
-    gathered = swap(grad, near(OUT2))
+    gathered = lax.all_to_all(
+        grad.reshape(-1, heads, width), "ctx", 0, 0, axis_index_groups=near(OUT2), tiled=True
+    ).reshape(grad.shape)
     suf, totals = call(
         near_suffix_kernel, "near_suffix", [shape(chunks), shape((groups, padded, width))], [gathered]
     )
+    totals = swap(totals, far(FAR2))
+    totals, dh = lax.optimization_barrier((totals, dh))
+    (after,) = call(
+        far_suffix_kernel, "far_suffix", [shape((members, 2 * chunk, width))], [totals, suf]
+    )
+    after = swap(after, near(BACK2))
     d_query, normed, dk, dv = call(
         back_kernel,
         "back",
@@ -416,12 +434,6 @@
         hbm_outs=(0, 1),
         aliases={8: 0, 9: 1},
     )
-    totals, normed, d_query, dk, dv = lax.optimization_barrier((totals, normed, d_query, dk, dv))
-    totals = swap(totals, far(FAR2))
-    (after,) = call(
-        far_suffix_kernel, "far_suffix", [shape((members, 2 * chunk, width))], [totals, suf]
-    )
-    after = swap(after, near(BACK2))
     d_key, d_value, d_state, d_gain = call(
         last_kernel,
         "last",

time: 105 us -> 105 us (level)
  starting transfers between devices: 9.87 us -> 20.3 us
  blocking collectives: 71.2 us -> 63.4 us
  waiting for transfers between devices: 13.2 us -> 9.31 us
    all_to_all x4 -> x3, blocking collectives: 63.9 us -> 43.4 us  [swap(): return lax.all_to_all(x, 'ctx', 0, 0, axis_index_groups=lists)]
    all_to_all x0 -> x1, blocking collectives: none -> 12.6 us  [on_device(): lax.all_to_all(grad.reshape(-1, heads, width), 'ctx', 0, 0, axis_index_gr...]
    all_to_all x2, starting transfers between devices: 9.87 us -> 20.3 us  [swap(): return lax.all_to_all(x, 'ctx', 0, 0, axis_index_groups=lists)]
    all_to_all x2, waiting for transfers between devices: 13.2 us -> 9.31 us  [swap(): return lax.all_to_all(x, 'ctx', 0, 0, axis_index_groups=lists)]
where the time goes in v5:
time: 105 us; the launch traced here: 104 us
  blocking collectives  63.4 us (60%)
  starting transfers between devices  20.3 us (19%)
  waiting for transfers between devices  9.31 us (9%)
  Pallas kernels  8.55 us (8%)
  local copies, waits for them, and re-layouts  1.91 us (2%)
    all_to_all x3, blocking collectives, swap(): return lax.all_to_all(x, 'ctx', 0, 0, axis_index_groups=lists)  43.4 us
    all_to_all x2, starting transfers between devices, swap(): return lax.all_to_all(x, 'ctx', 0, 0, axis_index_groups=lists)  20.3 us
    all_to_all x1, blocking collectives, on_device(): lax.all_to_all(grad.reshape(-1, heads, width), 'ctx', 0, 0, axis_index_gr...  12.6 us
    all_to_all x2, waiting for transfers between devices, swap(): return lax.all_to_all(x, 'ctx', 0, 0, axis_index_groups=lists)  9.31 us
    pallas_call x11, Pallas kernels, call(): pl.pallas_call(kernel, name=name, out_shape=outs, in_specs=places(len(arg...  8.55 us
    all_to_all x1, blocking collectives, on_device(): lax.all_to_all(stats, 'tp', 0, 0, axis_index_groups=[led_by(5, sharers)])  7.34 us
  transfers between devices with their start and end apart: 2, of which 2 were waited for; matrix products, arithmetic and copies ran while one was open for 0% of the time, Pallas kernels for 2%

profile of v5, /device:TPU:24, one launch (start us, length us, event | category | flops | bytes accessed | tf_op | source)
XLA Modules:
  0.0 104.1 jit_solution(70855142339494069)
XLA Ops:
  0.6 1.4 %state.1 = (f32[4,128,128]{2,1,0:T(8,128)S(1)}, bf16[4,256,128]{2,1,0:T(8,128)(2,1)S(1)}, bf16[4,256,128]{2,1,0:T(8,128)(2,1)S(1)}) custom-call(bf16[1024,128]{1,0:T(8,128)(2,1)} %bitcast.18, bf16[1024,128]{1,0:T(8,128)(2,1)} %bitcast.19), custom_call_target="tpu_custom_call" | custom-call | flops 33554432 | bytes 1310720 | tf_op jit(solution)/shard_map/state/pallas_call | solution.py:317
  2.0 15.7 %all_to_all.35.x_ref = f32[16,32,128]{2,1,0:T(8,128)S(1)} all-to-all(f32[16,32,128]{2,1,0:T(8,128)S(1)} %bitcast.14), channel_id=1, replica_groups={{80,0,8,16,24,32,40,48,56,64,72,88,96,104,112,120},{208,128,136,144,152..., dimensions={0} | all-to-all | bytes 524288 | tf_op jit(solution)/shard_map/all_to_all | solution.py:359
  17.7 0.7 near_prefix.1
  18.4 15.0 %all-to-all-start.1 = ((f32[4,32,128]{2,1,0:T(8,128)}), f32[4,32,128]{2,1,0:T(8,128)S(1)}, u32[]{:S(2)}, u32[]{:S(2)}) async-start(f32[4,32,128]{2,1,0:T(8,128)} %get-tuple-element.47), calls=%async_computation.1 | async-start | bytes 131072 | tf_op jit(solution)/shard_map/all_to_all | solution.py:359
  33.3 0.1 cotangent.1.ch_ref
  33.4 0.0 copy-start.5
  33.4 0.9 copy-done.3
  34.3 0.1 copy-done.4
  34.3 0.7 local.1
  35.0 0.9 all-to-all-done.1.totals_ref
  36.0 12.1 %all_to_all.36.before_ref = f32[16,32,128]{2,1,0:T(8,128)S(1)} all-to-all(f32[16,32,128]{2,1,0:T(8,128)S(1)} %far_prefix.1), channel_id=1, replica_groups={{48,0,8,16,24,32,40,56,64,72,80,88,96,104,112,120},{176,128,136,144,152..., dimensions={0} | all-to-all | bytes 524288 | tf_op jit(solution)/shard_map/all_to_all | solution.py:359
  48.1 0.4 attn.1
  48.5 7.3 %all_to_all.37.stats_ref = f32[8,4,128]{2,1,0:T(4,128)S(1)} all-to-all(f32[8,4,128]{2,1,0:T(4,128)S(1)} %get-tuple-element.64), channel_id=1, replica_groups={{5,0,1,2,3,4,6,7},{13,8,9,10,11,12,14,15},{21,16,17,18,19,20,22,23},{29..., dimensions={0} | all-to-all | bytes 32768 | tf_op jit(solution)/shard_map/all_to_all | solution.py:398
  55.8 2.0 %grad.1 = (bf16[4,256,128]{2,1,0:T(8,128)(2,1)S(1)}, f32[576,128]{1,0:T(8,128)S(1)}, f32[1,256]{1,0:T(1,128)S(1)}, bf16[1024,128]{1,0:T(8,128)(2,1)}, bf16[1024,128]{1,0:T(8,128)(2,1)}) custom-call(f32[8,4,128]{2,1,0:T(4,128)S(1)} %all_to_all.37.stats_ref, f32[4,256,128]{2,1,0:T(8,128)S(1)} %get-tuple-element.65.attn_ref, ...), custom_call_target="tpu_custom_call" | custom-call | flops 167772160 | bytes 2935808 | tf_op jit(solution)/shard_map/grad/pallas_call | solution.py:317
  57.8 0.0 copy-start
  57.8 12.6 %all_to_all.38 = f32[144,4,128]{2,1,0:T(4,128)S(1)} all-to-all(f32[144,4,128]{2,1,0:T(4,128)S(1)} %bitcast.12), channel_id=1, replica_groups={{48,0,8,16,24,32,40,56,64,72,80,88,96,104,112,120},{176,128,136,144,152..., dimensions={0} | all-to-all | bytes 589824 | tf_op jit(solution)/shard_map/all_to_all | solution.py:414
  70.5 0.0 copy-done
  70.5 15.6 %all_to_all.39.totals_ref = f32[4,40,128]{2,1,0:T(8,128)S(1)} all-to-all(f32[4,40,128]{2,1,0:T(8,128)S(1)} %get-tuple-element.68), channel_id=1, replica_groups={{256,0,384,128},{264,8,392,136},{272,16,400,144},{280,24,408,152},{288,..., dimensions={0} | all-to-all | bytes 163840 | tf_op jit(solution)/shard_map/all_to_all | solution.py:359
  86.1 0.8 far_suffix.1
  87.0 5.3 %all-to-all-start.6 = ((f32[16,64,128]{2,1,0:T(8,128)}), f32[16,64,128]{2,1,0:T(8,128)S(1)}, u32[]{:S(2)}, u32[]{:S(2)}) async-start(f32[16,64,128]{2,1,0:T(8,128)} %far_suffix.1), calls=%async_computation.6 | async-start | bytes 1048576 | tf_op jit(solution)/shard_map/all_to_all | solution.py:359
  92.3 0.9 copy-done.1
  93.3 1.1 %back.1 = (bf16[1024,128]{1,0:T(8,128)(2,1)}, bf16[1024,128]{1,0:T(8,128)(2,1)}, f32[4,256,128]{2,1,0:T(8,128)S(1)}, f32[4,256,128]{2,1,0:T(8,128)S(1)}) custom-call(bf16[4,256,128]{2,1,0:T(8,128)(2,1)S(1)} %copy-done.1, bf16[4,256,128]{2,1,0:T(8,128)(2,1)S(1)} %get-tuple-element.50.vh_ref, ...), custom_call_target="tpu_custom_call", output_to_operand_aliasing={{0}: (8, {}), {1}: (9, {})} | custom-call | flops 335544320 | bytes 3935232 | tf_op jit(solution)/shard_map/back/pallas_call | solution.py:317
  94.4 8.4 %all-to-all-done.6.after_ref = f32[16,64,128]{2,1,0:T(8,128)S(1)} async-done(((f32[16,64,128]{2,1,0:T(8,128)}), f32[16,64,128]{2,1,0:T(8,128)S(1)}, u32[]{:S(2)}, u32[]{:S(2)}) %all-to-all-start.6) | async-done | bytes 524320 | tf_op jit(solution)/shard_map/all_to_all | solution.py:359
  102.8 1.4 %last.1 = (bf16[1024,128]{1,0:T(8,128)(2,1)}, bf16[1024,128]{1,0:T(8,128)(2,1)}, f32[4,128,128]{2,1,0:T(8,128)}, f32[4,128]{1,0:T(4,128)}) custom-call(f32[16,64,128]{2,1,0:T(8,128)S(1)} %all-to-all-done.6.after_ref, f32[4,40,128]{2,1,0:T(8,128)S(1)} %all_to_all.39.totals_ref, bf16[4,256,128]{2,1,0:T(8,128)(2,1)S(1)} %get-tuple-element.49.kh_ref, ...), custom_call_target="tpu_custom_call" | custom-call | flops 134217728 | bytes 2967552 | tf_op jit(solution)/shard_map/last/pallas_call | solution.py:317
  (8 shorter events, 0.1 us)
Async XLA Ops:
  17.7 15.6 %copy-start.2 = (bf16[256,4,128]{2,1,0:T(4,128)(2,1)S(1)}, bf16[256,4,128]{2,1,0:T(4,128)(2,1)}, u32[]{:S(2)}) copy-start(bf16[256,4,128]{2,1,0:T(4,128)(2,1)} %param.11) | copy-start | bytes 786436
  18.4 17.6 %all-to-all-start.1 = ((f32[4,32,128]{2,1,0:T(8,128)}), f32[4,32,128]{2,1,0:T(8,128)S(1)}, u32[]{:S(2)}, u32[]{:S(2)}) async-start(f32[4,32,128]{2,1,0:T(8,128)} %get-tuple-element.47), calls=%async_computation.1 | async-start | bytes 131072 | tf_op jit(solution)/shard_map/all_to_all | solution.py:359
  33.3 1.0 copy-start.3
  33.3 1.0 copy-start.4
  33.4 1.0 copy-start.5
  57.8 12.7 %copy-start = (bf16[4,256,128]{2,1,0:T(8,128)(2,1)}, bf16[4,256,128]{2,1,0:T(8,128)(2,1)S(1)}, u32[]{:S(2)}) copy-start(bf16[4,256,128]{2,1,0:T(8,128)(2,1)S(1)} %get-tuple-element.70.dh_ref) | copy-start | bytes 786436
  87.0 15.8 %all-to-all-start.6 = ((f32[16,64,128]{2,1,0:T(8,128)}), f32[16,64,128]{2,1,0:T(8,128)S(1)}, u32[]{:S(2)}, u32[]{:S(2)}) async-start(f32[16,64,128]{2,1,0:T(8,128)} %far_suffix.1), calls=%async_computation.6 | async-start | bytes 1048576 | tf_op jit(solution)/shard_map/all_to_all | solution.py:359
  92.3 0.9 copy-start.1

commit v6 on v5

--- a/solution.py
+++ b/solution.py
@@ -417,12 +417,6 @@
     suf, totals = call(
         near_suffix_kernel, "near_suffix", [shape(chunks), shape((groups, padded, width))], [gathered]
     )
-    totals = swap(totals, far(FAR2))
-    totals, dh = lax.optimization_barrier((totals, dh))
-    (after,) = call(
-        far_suffix_kernel, "far_suffix", [shape((members, 2 * chunk, width))], [totals, suf]
-    )
-    after = swap(after, near(BACK2))
     d_query, normed, dk, dv = call(
         back_kernel,
         "back",
@@ -434,6 +428,12 @@
         hbm_outs=(0, 1),
         aliases={8: 0, 9: 1},
     )
+    totals, normed, d_query, dk, dv = lax.optimization_barrier((totals, normed, d_query, dk, dv))
+    totals = swap(totals, far(FAR2))
+    (after,) = call(
+        far_suffix_kernel, "far_suffix", [shape((members, 2 * chunk, width))], [totals, suf]
+    )
+    after = swap(after, near(BACK2))
     d_key, d_value, d_state, d_gain = call(
         last_kernel,
         "last",

time: 105 us -> 105 us (level)
  blocking collectives: 63.4 us -> 66.4 us
  waiting for transfers between devices: 9.31 us -> 7.96 us
    all_to_all x3 -> x4, blocking collectives: 43.4 us -> 59 us  [swap(): return lax.all_to_all(x, 'ctx', 0, 0, axis_index_groups=lists)]
    all_to_all x1 -> x0, blocking collectives: 12.6 us -> none  [on_device(): lax.all_to_all(grad.reshape(-1, heads, width), 'ctx', 0, 0, axis_index_gr...]
    all_to_all x2 -> x1, waiting for transfers between devices: 9.31 us -> 0.94 us  [swap(): return lax.all_to_all(x, 'ctx', 0, 0, axis_index_groups=lists)]
    all_to_all x0 -> x1, waiting for transfers between devices: none -> 7.01 us  [on_device(): lax.all_to_all(grad.reshape(-1, heads, width), 'ctx', 0, 0, axis_index_gr...]
    all_to_all x2 -> x1, starting transfers between devices: 20.3 us -> 15 us  [swap(): return lax.all_to_all(x, 'ctx', 0, 0, axis_index_groups=lists)]
    all_to_all x0 -> x1, starting transfers between devices: none -> 4.7 us  [on_device(): lax.all_to_all(grad.reshape(-1, heads, width), 'ctx', 0, 0, axis_index_gr...]
where the time goes in v6:
time: 105 us; the launch traced here: 104 us
  blocking collectives  66.4 us (63%)
  starting transfers between devices  19.7 us (19%)
  Pallas kernels  8.44 us (8%)
  waiting for transfers between devices  7.96 us (8%)
    all_to_all x4, blocking collectives, swap(): return lax.all_to_all(x, 'ctx', 0, 0, axis_index_groups=lists)  59 us
    all_to_all x1, starting transfers between devices, swap(): return lax.all_to_all(x, 'ctx', 0, 0, axis_index_groups=lists)  15 us
    pallas_call x11, Pallas kernels, call(): pl.pallas_call(kernel, name=name, out_shape=outs, in_specs=places(len(arg...  8.44 us
    all_to_all x1, blocking collectives, on_device(): lax.all_to_all(stats, 'tp', 0, 0, axis_index_groups=[led_by(5, sharers)])  7.34 us
    all_to_all x1, waiting for transfers between devices, on_device(): lax.all_to_all(grad.reshape(-1, heads, width), 'ctx', 0, 0, axis_index_gr...  7.01 us
    all_to_all x1, starting transfers between devices, on_device(): lax.all_to_all(grad.reshape(-1, heads, width), 'ctx', 0, 0, axis_index_gr...  4.7 us
  transfers between devices with their start and end apart: 2, of which 2 were waited for; matrix products, arithmetic and copies ran while one was open for 0% of the time, Pallas kernels for 2%

profile of v6, /device:TPU:24, one launch (start us, length us, event | category | flops | bytes accessed | tf_op | source)
XLA Modules:
  0.0 104.1 jit_solution(3923932058896059807)
XLA Ops:
  0.6 1.4 %state.1 = (f32[4,128,128]{2,1,0:T(8,128)S(1)}, bf16[4,256,128]{2,1,0:T(8,128)(2,1)S(1)}, bf16[4,256,128]{2,1,0:T(8,128)(2,1)S(1)}) custom-call(bf16[1024,128]{1,0:T(8,128)(2,1)} %bitcast.17, bf16[1024,128]{1,0:T(8,128)(2,1)} %bitcast.18), custom_call_target="tpu_custom_call" | custom-call | flops 33554432 | bytes 1310720 | tf_op jit(solution)/shard_map/state/pallas_call | solution.py:317
  2.0 15.7 %all_to_all.35.x_ref = f32[16,32,128]{2,1,0:T(8,128)S(1)} all-to-all(f32[16,32,128]{2,1,0:T(8,128)S(1)} %bitcast.13), channel_id=1, replica_groups={{80,0,8,16,24,32,40,48,56,64,72,88,96,104,112,120},{208,128,136,144,152..., dimensions={0} | all-to-all | bytes 524288 | tf_op jit(solution)/shard_map/all_to_all | solution.py:359
  17.7 0.0 copy-start
  17.7 0.7 near_prefix.1
  18.4 15.0 %all-to-all-start.1 = ((f32[4,32,128]{2,1,0:T(8,128)}), f32[4,32,128]{2,1,0:T(8,128)S(1)}, u32[]{:S(2)}, u32[]{:S(2)}) async-start(f32[4,32,128]{2,1,0:T(8,128)} %get-tuple-element.50), calls=%async_computation.1 | async-start | bytes 131072 | tf_op jit(solution)/shard_map/all_to_all | solution.py:359
  33.3 0.0 copy-done
  33.3 0.0 copy-start.1
  33.3 0.1 cotangent.1.ch_ref
  33.4 0.0 copy-start.3
  33.4 0.9 copy-done.1
  34.3 0.1 copy-done.2
  34.3 0.0 copy-done.3
  34.3 0.7 local.1
  35.0 0.9 all-to-all-done.1.totals_ref
  36.0 12.1 %all_to_all.36.before_ref = f32[16,32,128]{2,1,0:T(8,128)S(1)} all-to-all(f32[16,32,128]{2,1,0:T(8,128)S(1)} %far_prefix.1), channel_id=1, replica_groups={{48,0,8,16,24,32,40,56,64,72,80,88,96,104,112,120},{176,128,136,144,152..., dimensions={0} | all-to-all | bytes 524288 | tf_op jit(solution)/shard_map/all_to_all | solution.py:359
  48.1 0.4 attn.1
  48.5 7.3 %all_to_all.37.stats_ref = f32[8,4,128]{2,1,0:T(4,128)S(1)} all-to-all(f32[8,4,128]{2,1,0:T(4,128)S(1)} %get-tuple-element.67), channel_id=1, replica_groups={{5,0,1,2,3,4,6,7},{13,8,9,10,11,12,14,15},{21,16,17,18,19,20,22,23},{29..., dimensions={0} | all-to-all | bytes 32768 | tf_op jit(solution)/shard_map/all_to_all | solution.py:398
  55.8 2.7 %grad.1 = (bf16[4,256,128]{2,1,0:T(8,128)(2,1)S(1)}, f32[576,128]{1,0:T(8,128)}, f32[1,256]{1,0:T(1,128)S(1)}, bf16[1024,128]{1,0:T(8,128)(2,1)}, bf16[1024,128]{1,0:T(8,128)(2,1)}) custom-call(f32[8,4,128]{2,1,0:T(4,128)S(1)} %all_to_all.37.stats_ref, f32[4,256,128]{2,1,0:T(8,128)S(1)} %get-tuple-element.68.attn_ref, ...), custom_call_target="tpu_custom_call" | custom-call | flops 167772160 | bytes 2935808 | tf_op jit(solution)/shard_map/grad/pallas_call | solution.py:317
  58.5 4.7 %all-to-all-start.4 = ((f32[144,4,128]{2,1,0:T(4,128)}), f32[144,4,128]{2,1,0:T(4,128)S(1)}, u32[]{:S(2)}, u32[]{:S(2)}) async-start(f32[144,4,128]{2,1,0:T(4,128)} %bitcast.5), calls=%async_computation.4 | async-start | bytes 589824 | tf_op jit(solution)/shard_map/all_to_all | solution.py:414
  63.2 1.1 %back.1 = (bf16[1024,128]{1,0:T(8,128)(2,1)}, bf16[1024,128]{1,0:T(8,128)(2,1)}, f32[4,256,128]{2,1,0:T(8,128)S(1)}, f32[4,256,128]{2,1,0:T(8,128)S(1)}) custom-call(bf16[4,256,128]{2,1,0:T(8,128)(2,1)S(1)} %get-tuple-element.72.dh_ref, bf16[4,256,128]{2,1,0:T(8,128)(2,1)S(1)} %get-tuple-element.53.vh_ref, ...), custom_call_target="tpu_custom_call", output_to_operand_aliasing={{0}: (8, {}), {1}: (9, {})} | custom-call | flops 335544320 | bytes 3935232 | tf_op jit(solution)/shard_map/back/pallas_call | solution.py:317
  64.4 7.0 %all-to-all-done.4 = f32[144,4,128]{2,1,0:T(4,128)S(1)} async-done(((f32[144,4,128]{2,1,0:T(4,128)}), f32[144,4,128]{2,1,0:T(4,128)S(1)}, u32[]{:S(2)}, u32[]{:S(2)}) %all-to-all-start.4) | async-done | bytes 294944 | tf_op jit(solution)/shard_map/all_to_all | solution.py:414
  71.4 15.6 %all_to_all.38.totals_ref = f32[4,40,128]{2,1,0:T(8,128)S(1)} all-to-all(f32[4,40,128]{2,1,0:T(8,128)S(1)} %get-tuple-element.82), channel_id=1, replica_groups={{256,0,384,128},{264,8,392,136},{272,16,400,144},{280,24,408,152},{288,..., dimensions={0} | all-to-all | bytes 163840 | tf_op jit(solution)/shard_map/all_to_all | solution.py:359
  87.1 15.6 %all_to_all.39.after_ref = f32[16,64,128]{2,1,0:T(8,128)S(1)} all-to-all(f32[16,64,128]{2,1,0:T(8,128)S(1)} %far_suffix.1), channel_id=1, replica_groups={{80,0,8,16,24,32,40,48,56,64,72,88,96,104,112,120},{208,128,136,144,152..., dimensions={0} | all-to-all | bytes 1048576 | tf_op jit(solution)/shard_map/all_to_all | solution.py:359
  102.7 1.3 %last.1 = (bf16[1024,128]{1,0:T(8,128)(2,1)}, bf16[1024,128]{1,0:T(8,128)(2,1)}, f32[4,128,128]{2,1,0:T(8,128)}, f32[4,128]{1,0:T(4,128)}) custom-call(f32[16,64,128]{2,1,0:T(8,128)S(1)} %all_to_all.39.after_ref, f32[4,40,128]{2,1,0:T(8,128)S(1)} %all_to_all.38.totals_ref, bf16[4,256,128]{2,1,0:T(8,128)(2,1)S(1)} %get-tuple-element.52.kh_ref, ...), custom_call_target="tpu_custom_call" | custom-call | flops 134217728 | bytes 2967552 | tf_op jit(solution)/shard_map/last/pallas_call | solution.py:317
  (4 shorter events, 0.1 us)
Async XLA Ops:
  17.7 15.6 %copy-start = (bf16[256,4,128]{2,1,0:T(4,128)(2,1)S(1)}, bf16[256,4,128]{2,1,0:T(4,128)(2,1)}, u32[]{:S(2)}) copy-start(bf16[256,4,128]{2,1,0:T(4,128)(2,1)} %param.11) | copy-start | bytes 786436
  18.4 17.6 %all-to-all-start.1 = ((f32[4,32,128]{2,1,0:T(8,128)}), f32[4,32,128]{2,1,0:T(8,128)S(1)}, u32[]{:S(2)}, u32[]{:S(2)}) async-start(f32[4,32,128]{2,1,0:T(8,128)} %get-tuple-element.50), calls=%async_computation.1 | async-start | bytes 131072 | tf_op jit(solution)/shard_map/all_to_all | solution.py:359
  33.3 1.0 copy-start.1
  33.3 1.0 copy-start.2
  33.4 1.0 copy-start.3
  58.5 12.9 %all-to-all-start.4 = ((f32[144,4,128]{2,1,0:T(4,128)}), f32[144,4,128]{2,1,0:T(4,128)S(1)}, u32[]{:S(2)}, u32[]{:S(2)}) async-start(f32[144,4,128]{2,1,0:T(4,128)} %bitcast.5), calls=%async_computation.4 | async-start | bytes 589824 | tf_op jit(solution)/shard_map/all_to_all | solution.py:414
